TPU v7x, 256 devices: a whole 4x4x8 slice. The times are simulated.
256 devices in a mesh: scene: 16 (over z_hi, x), view: 16 (over y, z_lo, core).
Axes of the slice: x: 4, y: 4, z: 8 (z_hi: 4, z_lo: 2; z = z_hi * 2 + z_lo), core: 2. Of those that a mesh axis runs over, the one named last changes fastest.
Arguments:
- keys: bfloat16 [32768, 1024], P(('scene', 'view')), parts along dimension 0, may hold values from -6 to 6
- values: bfloat16 [32768, 1024], P(('scene', 'view')), parts along dimension 0, may hold values from -6 to 6
- rates: bfloat16 [32768, 16], P(('scene', 'view')), parts along dimension 0, may hold values from 0.099609375 to 1
- queries: bfloat16 [16384, 1024], P(('scene', 'view')), parts along dimension 0, may hold values from -6 to 6
- gate_up: bfloat16 [2, 16, 64, 1024], P(None, None, None, 'view'), may hold values from -0.75 to 0.75
- down_t: bfloat16 [16, 64, 1024], P(None, None, 'view'), may hold values from -0.1875 to 0.1875
- step_sizes: float32 [16], replicated, may hold values from 1 to 4
- gain: float32 [1024], replicated, may hold values from 0.1 to 1.9
Outputs:
- outputs: bfloat16 [16384, 1024], P(('scene', 'view')), parts along dimension 0
There are 16 independent parts, one for each index of `scene`. A program takes and returns all parts, laid end to end along the dimension named above; an argument that names none is the same for every part. Nothing has to cross between parts.
All inputs are finite; a program needn't handle non-finite values.
Results may differ from a plain program's by a relative error of at most 0.0083.
Values may be sent and summed in bfloat16 or wider, within the bound.
A program may use at most 128 MiB of HBM per device.

v0:
```python
import jax
import jax.numpy as jnp
from jax import lax
from jax.sharding import PartitionSpec as P

NS_STEPS = 5


poly_one = 3.4445
poly_two = -4.775
poly_three = 2.0315


def grad_terms(key_rows, value_rows, rate_rows, gate_w, up_w, down_w):
    count = key_rows.shape[0]
    heads = rate_rows.shape[1]
    key_heads = key_rows.reshape(count, heads, -1)
    value_heads = value_rows.reshape(count, heads, -1)
    pre_gate = jnp.einsum("thd,hdf->htf", key_heads, gate_w, preferred_element_type=jnp.float32)
    pre_up = jnp.einsum("thd,hdf->htf", key_heads, up_w, preferred_element_type=jnp.float32)
    sigma = jax.nn.sigmoid(pre_gate)
    gated = pre_gate * sigma
    hidden = (gated * pre_up).astype(jnp.bfloat16)
    out_grad = (
        -(rate_rows.astype(jnp.float32)[:, :, None] * value_heads.astype(jnp.float32))
    ).astype(jnp.bfloat16)
    down_grad = jnp.einsum("thd,htf->hdf", out_grad, hidden, preferred_element_type=jnp.float32)
    hidden_grad = jnp.einsum("thd,hdf->htf", out_grad, down_w, preferred_element_type=jnp.float32)
    gate_term = (hidden_grad * pre_up * sigma * (1.0 + pre_gate * (1.0 - sigma))).astype(
        jnp.bfloat16
    )
    up_term = (hidden_grad * gated).astype(jnp.bfloat16)
    gate_grad = jnp.einsum("thd,htf->hdf", key_heads, gate_term, preferred_element_type=jnp.float32)
    up_grad = jnp.einsum("thd,htf->hdf", key_heads, up_term, preferred_element_type=jnp.float32)
    return jnp.stack([gate_grad, up_grad, down_grad])


def local_gram(current):
    return jnp.einsum("mhik,mhjk->mhij", current, current, precision=lax.Precision.HIGHEST)


def summed_gram(current):
    return lax.psum(local_gram(current), "view")


def orthogonalize(grads, gram_fn):
    gram = gram_fn(grads)
    square_norm = jnp.trace(gram, axis1=2, axis2=3)[:, :, None, None]
    factor = 1.0 / (jnp.sqrt(square_norm) + 1e-07)
    current = grads * factor
    gram = gram * (factor * factor)
    for step in range(NS_STEPS):
        if step > 0:
            gram = gram_fn(current)
        square = jnp.einsum("mhij,mhjk->mhik", gram, gram, precision=lax.Precision.HIGHEST)
        blend = poly_two * gram + poly_three * square
        current = poly_one * current + jnp.einsum(
            "mhij,mhjk->mhik", blend, current, precision=lax.Precision.HIGHEST
        )
    return current


def renew_weights(grads, stacked, head_steps, gram_fn):
    weights = stacked.astype(jnp.float32)
    moved = weights - head_steps[None, :, None, None] * orthogonalize(grads, gram_fn)
    keep = jnp.sqrt(jnp.sum(weights * weights, axis=2, keepdims=True))
    length = jnp.sqrt(jnp.sum(moved * moved, axis=2, keepdims=True))
    return (moved * (keep / (length + 1e-06))).astype(jnp.bfloat16)


def apply_heads(query_rows, fresh):
    count = query_rows.shape[0]
    heads = fresh.shape[1]
    query_heads = query_rows.reshape(count, heads, -1)
    query_gate = jnp.einsum(
        "thd,hdf->htf", query_heads, fresh[0], preferred_element_type=jnp.float32
    )
    query_up = jnp.einsum("thd,hdf->htf", query_heads, fresh[1], preferred_element_type=jnp.float32)
    query_hidden = (query_gate * jax.nn.sigmoid(query_gate) * query_up).astype(jnp.bfloat16)
    head_out = jnp.einsum(
        "htf,hdf->thd", query_hidden, fresh[2], preferred_element_type=jnp.float32
    )
    return head_out.reshape(count, -1)


def finish_norm(head_out, gain_part, heads):
    count = head_out.shape[0]
    shaped = head_out.reshape(count, heads, -1)
    mean_square = jnp.mean(shaped * shaped, axis=-1, keepdims=True)
    scaled = shaped * lax.rsqrt(mean_square + 1e-06) * gain_part.reshape(heads, -1)
    return scaled.astype(jnp.bfloat16).reshape(count, -1)


def shards(keys, values, rates, queries, gate_up, down_t, step_sizes, gain):
    heads = rates.shape[1]
    stacked = jnp.concatenate([gate_up, down_t[None]], axis=0)
    grads = grad_terms(
        lax.all_gather(keys, "view", axis=0, tiled=True),
        lax.all_gather(values, "view", axis=0, tiled=True),
        lax.all_gather(rates, "view", axis=0, tiled=True),
        stacked[0],
        stacked[1],
        stacked[2],
    )
    fresh = renew_weights(grads, stacked, step_sizes, summed_gram)
    terms = apply_heads(lax.all_gather(queries, "view", axis=0, tiled=True), fresh)
    summed = lax.psum_scatter(terms, "view", scatter_dimension=0, tiled=True)
    return finish_norm(summed, gain, heads)


def solution(mesh):
    return jax.shard_map(
        shards,
        mesh=mesh,
        in_specs=(
            P(("scene", "view"), None),
            P(("scene", "view"), None),
            P(("scene", "view"), None),
            P(("scene", "view"), None),
            P(None, None, None, "view"),
            P(None, None, "view"),
            P(),
            P(),
        ),
        out_specs=P(("scene", "view"), None),
        check_vma=False,
    )
```

profile of v0, /device:TPU:1, one launch (start us, length us, event | category | flops | bytes accessed | tf_op | source)
XLA Modules:
  0.0 945.5 jit_solution(2376880063557221838)
XLA Ops:
  6.5 0.7 all-gather.6.cloned.1.call-update
  7.3 0.0 all-gather.4.cloned.1.call-start
  7.3 1.8 copy.17
  9.1 0.0 all-gather.4.cloned.1.call-update
  9.1 0.0 all-reduce.6.cloned.1.call-start
  9.2 22.1 %all_gather.12 = bf16[2048,16]{0,1:T(8,128)(2,1)S(1)} all-gather(bf16[128,16]{0,1:T(8,128)(2,1)} %param.10), channel_id=1, replica_groups=mesh['scene'=16,'view'=16] {'view'}, dimensions={0}, use_global_device_ids=true | all-gather | bytes 69632 | tf_op jit(solution)/shard_map/all_gather | solution.py:100
  31.3 22.1 %all-gather.6.cloned.1.call-done = bf16[2048,1024]{1,0:T(8,128)(2,1)} async-done(((bf16[128,1024]{1,0:T(8,128)(2,1)}), bf16[2048,1024]{1,0:T(8,128)(2,1)}) %all-gather.6.cloned.1.call-update) | async-done | bytes 4194320 | tf_op jit(solution)/shard_map/all_gather | solution.py:98
  53.4 6.5 copy.19
  60.0 6.9 fusion.71
  66.8 4.5 fusion.73
  71.3 32.7 %all-gather.4.cloned.1.call-done = bf16[2048,1024]{0,1:T(8,128)(2,1)} async-done(((bf16[128,1024]{0,1:T(8,128)(2,1)}), bf16[2048,1024]{0,1:T(8,128)(2,1)}) %all-gather.4.cloned.1.call-update) | async-done | bytes 4194320 | tf_op jit(solution)/shard_map/all_gather | solution.py:99
  104.1 6.9 fusion.11
  110.9 7.5 fusion.55
  118.5 10.6 %fusion.51 = f32[1,16,64,64]{3,2,1,0:T(8,128)S(1)} fusion(bf16[2048,16,64]{0,2,1:T(8,128)(2,1)S(1)} %bitcast.87, f32[16,2048,64]{1,2,0:T(8,128)} %fusion.71, f32[16,2048,64]{1,2,0:T(8,128)} %fusion.11, f32[16,2048,64]{1,2,0:T(8,128)} %fusion.73), kind=kOutput, calls=%fused_computation.55 | convolution fusion | flops 289406976 | bytes 29622272 | tf_op jit(solution)/shard_map/thd,htf->hdf/dot_general | solution.py:33
  129.1 7.7 fusion.52
  136.8 3.7 fusion.56
  140.5 0.0 all-reduce.6.cloned.1.call-update
  140.5 0.6 all-reduce.8.cloned.1.call-start
  141.1 124.5 %all-reduce.6.cloned.1.call-done = f32[3,16,64,64]{3,2,1,0:T(8,128)} async-done(((f32[3,16,64,64]{3,2,1,0:T(8,128)}), f32[3,16,64,64]{3,2,1,0:T(8,128)}) %all-reduce.6.cloned.1.call-update) | async-done | bytes 786448 | tf_op jit(solution)/shard_map/psum | solution.py:43
  265.6 1.8 select_reduce_fusion
  267.4 0.0 copy-done.2
  267.5 1.9 fusion.46
  269.4 2.2 multiply_add_fusion.3
  271.6 3.7 fusion.94
  275.4 0.0 all-reduce.8.cloned.1.call-update
  275.4 0.2 all-reduce.10.cloned.1.call-start
  275.6 126.8 %all-reduce.8.cloned.1.call-done = f32[3,16,64,64]{3,2,1,0:T(8,128)} async-done(((f32[3,16,64,64]{3,2,1,0:T(8,128)}), f32[3,16,64,64]{3,2,1,0:T(8,128)}) %all-reduce.8.cloned.1.call-update) | async-done | bytes 786448 | tf_op jit(solution)/shard_map/psum | solution.py:43
  402.4 3.8 fusion.95
  406.2 1.9 multiply_add_fusion.2
  408.1 3.7 fusion.96
  411.9 0.0 all-reduce.10.cloned.1.call-update
  411.9 0.3 all-reduce.12.cloned.1.call-start
  412.2 126.8 %all-reduce.10.cloned.1.call-done = f32[3,16,64,64]{3,2,1,0:T(8,128)} async-done(((f32[3,16,64,64]{3,2,1,0:T(8,128)}), f32[3,16,64,64]{3,2,1,0:T(8,128)}) %all-reduce.10.cloned.1.call-update) | async-done | bytes 786448 | tf_op jit(solution)/shard_map/psum | solution.py:43
  539.0 3.8 fusion.97
  542.8 1.9 multiply_add_fusion.1
  544.7 3.8 fusion.98
  548.5 0.0 all-gather.8.cloned.1.call-start
  548.5 0.7 all-gather.8.cloned.1.call-update
  549.2 0.3 all-reduce.14.cloned.1.call-start
  549.5 126.0 %all-reduce.12.cloned.1.call-done = f32[3,16,64,64]{3,2,1,0:T(8,128)} async-done(((f32[3,16,64,64]{3,2,1,0:T(8,128)}), f32[3,16,64,64]{3,2,1,0:T(8,128)}) %all-reduce.12.cloned.1.call-update) | async-done | bytes 786448 | tf_op jit(solution)/shard_map/psum | solution.py:43
  675.5 3.7 fusion.99
  679.2 1.9 multiply_add_fusion
  681.1 3.8 fusion.100
  684.9 0.3 reduce-scatter.2.cloned.1.call-start
  685.2 0.7 copy-done.9
  685.9 0.3 fusion.14
  686.2 28.7 %all-gather.8.cloned.1.call-done = bf16[1024,1024]{1,0:T(8,128)(2,1)} async-done(((bf16[64,1024]{1,0:T(8,128)(2,1)}), bf16[1024,1024]{1,0:T(8,128)(2,1)}) %all-gather.8.cloned.1.call-update) | async-done | bytes 2097168 | tf_op jit(solution)/shard_map/all_gather | solution.py:106
  715.0 3.9 copy.22
  718.9 124.5 %all-reduce.14.cloned.1.call-done = f32[3,16,64,64]{3,2,1,0:T(8,128)} async-done(((f32[3,16,64,64]{3,2,1,0:T(8,128)}), f32[3,16,64,64]{3,2,1,0:T(8,128)}) %all-reduce.14.cloned.1.call-update) | async-done | bytes 786448 | tf_op jit(solution)/shard_map/psum | solution.py:43
  843.4 3.7 fusion.101
  847.1 2.3 multiply_reduce_fusion
  849.5 0.2 multiply_convert_fusion.6
  849.7 1.3 copy-done.7
  851.0 2.7 fusion.70
  853.8 6.3 fusion.13
  860.1 5.4 copy.24
  865.5 70.3 %reduce-scatter.2.cloned.1.call-done = f32[64,1024]{1,0:T(8,128)} async-done(((f32[1024,1024]{1,0:T(8,128)}), f32[64,1024]{1,0:T(8,128)}) %reduce-scatter.2.cloned.1.call-update) | async-done | bytes 262160 | tf_op jit(solution)/shard_map/reduce_scatter | solution.py:107
  935.8 1.1 mul.189
  936.9 0.1 mul.190
  937.0 0.2 reduce_sum.40
  937.2 0.2 mul.191
  937.4 0.2 mul.192
  937.6 0.2 copy-done.12
  937.8 0.7 multiply_convert_fusion.13
  (35 shorter events, 0.2 us)
Async XLA Ops:
  6.5 46.9 %all-gather.6.cloned.1.call-start = ((), (), s32[]{:S(2)}) async-start(), calls=%async_computation.2 | async-start | bytes 4456448 | tf_op jit(solution)/shard_map/all_gather | solution.py:98
  7.3 96.8 %all-gather.4.cloned.1.call-start = ((), (), s32[]{:S(2)}) async-start(), calls=%async_computation.1 | async-start | bytes 4456448 | tf_op jit(solution)/shard_map/all_gather | solution.py:99
  9.1 256.5 %all-reduce.6.cloned.1.call-start = ((), (), s32[]{:S(2)}) async-start(), calls=%async_computation.3 | async-start | bytes 3145728 | tf_op jit(solution)/shard_map/psum | solution.py:43
  31.3 28.7 %copy-start.8 = (bf16[2,16,64,64]{3,2,1,0:T(8,128)(2,1)S(1)}, bf16[2,16,64,64]{3,2,1,0:T(8,128)(2,1)}, u32[]{:S(2)}) copy-start(bf16[2,16,64,64]{3,2,1,0:T(8,128)(2,1)} %param.12) | copy-start | bytes 786436
  59.9 6.9 copy-start
  66.8 37.2 %copy-start.11 = (bf16[16,64,64]{2,1,0:T(8,128)(2,1)S(1)}, bf16[16,64,64]{2,1,0:T(8,128)(2,1)}, u32[]{:S(2)}) copy-start(bf16[16,64,64]{2,1,0:T(8,128)(2,1)} %param.13) | copy-start | bytes 393220
  104.1 6.9 copy-start.1
  118.4 10.6 %copy-start.10 = (bf16[2048,1024]{0,1:T(8,128)(2,1)S(1)}, bf16[2048,1024]{0,1:T(8,128)(2,1)}, u32[]{:S(2)}) copy-start(bf16[2048,1024]{0,1:T(8,128)(2,1)} %all-gather.4.cloned.1.call-done) | copy-start | bytes 12582916
  140.5 261.9 %all-reduce.8.cloned.1.call-start = ((), (), s32[]{:S(2)}) async-start(), calls=%async_computation.4 | async-start | bytes 3145728 | tf_op jit(solution)/shard_map/psum | solution.py:43
  265.6 1.9 copy-start.2
  275.4 263.6 %all-reduce.10.cloned.1.call-start = ((), (), s32[]{:S(2)}) async-start(), calls=%async_computation.5 | async-start | bytes 3145728 | tf_op jit(solution)/shard_map/psum | solution.py:43
  402.4 3.8 copy-start.5
  411.9 263.6 %all-reduce.12.cloned.1.call-start = ((), (), s32[]{:S(2)}) async-start(), calls=%async_computation.6 | async-start | bytes 3145728 | tf_op jit(solution)/shard_map/psum | solution.py:43
  538.9 3.8 copy-start.6
  548.5 166.5 %all-gather.8.cloned.1.call-start = ((), (), s32[]{:S(2)}) async-start(), calls=%async_computation.8 | async-start | bytes 2228224 | tf_op jit(solution)/shard_map/all_gather | solution.py:106
  549.2 294.2 %all-reduce.14.cloned.1.call-start = ((), (), s32[]{:S(2)}) async-start(), calls=%async_computation.7 | async-start | bytes 3145728 | tf_op jit(solution)/shard_map/psum | solution.py:43
  675.5 3.7 copy-start.3
  684.9 1.0 copy-start.9
  684.9 250.9 %reduce-scatter.2.cloned.1.call-start = ((), (), s32[]{:S(2)}) async-start(), calls=%async_computation.9 | async-start | bytes 4456448 | tf_op jit(solution)/shard_map/reduce_scatter | solution.py:107
  718.9 128.2 %copy-start.14 = (f32[16]{0:T(128)S(1)}, f32[16]{0:T(128)}, u32[]{:S(2)}) copy-start(f32[16]{0:T(128)} %param.14) | copy-start | bytes 196
  843.4 3.7 copy-start.4
  849.4 1.6 copy-start.7
  936.8 1.0 copy-start.12
  936.9 0.9 copy-start.13
Sparse Core Ops, SparseCore 0:
  9.2 44.1 all-gather.5
  55.2 48.8 all-gather.3
  140.7 124.8 all-reduce.5
  275.5 126.8 all-reduce.7
  412.0 126.8 all-reduce.9
  548.6 126.8 all-reduce.11
  677.4 37.5 all-gather.7
  717.6 125.7 all-reduce.13
  865.6 70.1 reduce-scatter.1
where the time goes:
time: 956 us; the launch traced here: 946 us
  waiting for transfers between devices  784 us (82%)
  matrix products  99 us (10%)
  blocking collectives  22.1 us (2%)
  local copies, waits for them, and re-layouts  20.4 us (2%)
  between operations  14 us (1%)
    psum x5, waiting for transfers between devices, summed_gram(): return lax.psum(local_gram(current), 'view')  629 us
    reduce_scatter x1, waiting for transfers between devices, shards(): summed = lax.psum_scatter(terms, 'view', scatter_dimension=0, tiled=True)  70.3 us
    all_gather x1, waiting for transfers between devices, shards(): lax.all_gather(values, 'view', axis=0, tiled=True)  32.7 us
    all_gather x1, waiting for transfers between devices, shards(): lax.all_gather(queries, 'view', axis=0, tiled=True)  28.7 us
    all_gather x1, waiting for transfers between devices, shards(): lax.all_gather(keys, 'view', axis=0, tiled=True)  22.1 us
    all_gather x1, blocking collectives, shards(): lax.all_gather(rates, 'view', axis=0, tiled=True)  22.1 us
  transfers between devices with their start and end apart: 9, of which 9 were waited for; matrix products, arithmetic and copies ran while one was open for 4% of the time, Pallas kernels for 0%

commit v1 on v0

v1 whole, which is shorter than its diff:
```python
import jax
import jax.numpy as jnp
from jax import lax
from jax.sharding import PartitionSpec as P

NS_STEPS = 5


poly_one = 3.4445
poly_two = -4.775
poly_three = 2.0315


def exact_dot(left, right):
    return jnp.einsum("mij,mjk->mik", left, right, precision=lax.Precision.HIGHEST)


def fast_dot(spec, left, right):
    return jnp.einsum(spec, left, right, preferred_element_type=jnp.float32)


def grad_terms(keys, out_grad, gate_w, up_w, down_w):
    pre_gate = fast_dot("td,df->tf", keys, gate_w)
    pre_up = fast_dot("td,df->tf", keys, up_w)
    sigma = jax.nn.sigmoid(pre_gate)
    gated = pre_gate * sigma
    hidden = (gated * pre_up).astype(jnp.bfloat16)
    down_grad = fast_dot("td,tf->df", out_grad, hidden)
    hidden_grad = fast_dot("td,df->tf", out_grad, down_w)
    gate_term = (hidden_grad * pre_up * sigma * (1.0 + pre_gate * (1.0 - sigma))).astype(
        jnp.bfloat16
    )
    up_term = (hidden_grad * gated).astype(jnp.bfloat16)
    gate_grad = fast_dot("td,tf->df", keys, gate_term)
    up_grad = fast_dot("td,tf->df", keys, up_term)
    return jnp.stack([gate_grad, up_grad, down_grad])


def orthogonalize(grads):
    gram = jnp.einsum("mik,mjk->mij", grads, grads, precision=lax.Precision.HIGHEST)
    square_norm = jnp.trace(gram, axis1=1, axis2=2)[:, None, None]
    factor = 1.0 / (jnp.sqrt(square_norm) + 1e-07)
    gram = gram * (factor * factor)
    eye = jnp.eye(gram.shape[1], dtype=jnp.float32)
    total = None
    for step in range(NS_STEPS):
        square = exact_dot(gram, gram)
        blend = poly_one * eye + poly_two * gram + poly_three * square
        total = blend if total is None else exact_dot(blend, total)
        if step < NS_STEPS - 1:
            gram = exact_dot(exact_dot(blend, gram), blend)
    return exact_dot(total * factor, grads)


def renew_weights(grads, stacked, head_step):
    weights = stacked.astype(jnp.float32)
    moved = weights - head_step * orthogonalize(grads)
    keep = jnp.sqrt(jnp.sum(weights * weights, axis=1, keepdims=True))
    length = jnp.sqrt(jnp.sum(moved * moved, axis=1, keepdims=True))
    return (moved * (keep / (length + 1e-06))).astype(jnp.bfloat16)


def apply_head(queries, fresh, gain):
    query_gate = fast_dot("td,df->tf", queries, fresh[0])
    query_up = fast_dot("td,df->tf", queries, fresh[1])
    query_hidden = (query_gate * jax.nn.sigmoid(query_gate) * query_up).astype(jnp.bfloat16)
    head_out = fast_dot("tf,df->td", query_hidden, fresh[2])
    mean_square = jnp.mean(head_out * head_out, axis=-1, keepdims=True)
    return (head_out * lax.rsqrt(mean_square + 1e-06) * gain).astype(jnp.bfloat16)


def to_heads(rows, heads):
    count = rows.shape[0]
    split = rows.reshape(count, heads, -1).transpose(1, 0, 2)
    moved = lax.all_to_all(split, "view", split_axis=0, concat_axis=0, tiled=True)
    return moved.reshape(heads * count, -1)


def shards(keys, values, rates, queries, gate_up, down_t, step_sizes, gain):
    heads = rates.shape[1]
    mine = lax.axis_index("view")
    value_heads = values.reshape(values.shape[0], heads, -1).astype(jnp.float32)
    out_grad = (-(rates.astype(jnp.float32)[:, :, None] * value_heads)).astype(jnp.bfloat16)
    stacked = jnp.concatenate([gate_up, down_t[None]], axis=0)
    stacked = lax.all_to_all(stacked, "view", split_axis=1, concat_axis=3, tiled=True)[:, 0]
    grads = grad_terms(
        to_heads(keys, heads),
        to_heads(out_grad.reshape(values.shape), heads),
        stacked[0],
        stacked[1],
        stacked[2],
    )
    fresh = renew_weights(grads, stacked, step_sizes[mine])
    head_gain = lax.dynamic_slice_in_dim(gain.reshape(heads, -1), mine, 1)
    result = apply_head(to_heads(queries, heads), fresh, head_gain)
    count = queries.shape[0]
    back = lax.all_to_all(
        result.reshape(heads, count, -1), "view", split_axis=0, concat_axis=0, tiled=True
    )
    return back.transpose(1, 0, 2).reshape(count, -1)


def solution(mesh):
    return jax.shard_map(
        shards,
        mesh=mesh,
        in_specs=(
            P(("scene", "view"), None),
            P(("scene", "view"), None),
            P(("scene", "view"), None),
            P(("scene", "view"), None),
            P(None, None, None, "view"),
            P(None, None, "view"),
            P(),
            P(),
        ),
        out_specs=P(("scene", "view"), None),
        check_vma=False,
    )
```

time: 956 us -> 98.3 us (0.10); the launches traced: 946 us -> 97.6 us
  waiting for transfers between devices: 784 us -> 11.2 us
  matrix products: 99 us -> 35.2 us
  starting transfers between devices: 1.78 us -> 20.1 us
  between operations: 14 us -> 0.4 us
  blocking collectives: 22.1 us -> 11.7 us
    psum x5 -> x0, waiting for transfers between devices: 629 us -> none  [summed_gram(): return lax.psum(local_gram(current), 'view')]
    all_gather x3 -> x0, waiting for transfers between devices: 83.6 us -> none  [the longest x1 32.7 us: shards(): lax.all_gather(values, 'view', axis=0, tiled=True)]
    reduce_scatter x1 -> x0, waiting for transfers between devices: 70.3 us -> none  [shards(): summed = lax.psum_scatter(terms, 'view', scatter_dimension=0, tiled=True)]
    dot_general x23 -> x27, matrix products: 99 us -> 35.2 us  [the longest x8 27.8 us: fast_dot(): return jnp.einsum(spec, left, right, preferred_element_type=jnp.float32)]
    all_gather x1 -> x0, blocking collectives: 22.1 us -> none  [shards(): lax.all_gather(rates, 'view', axis=0, tiled=True)]
    all_to_all x0 -> x4, starting transfers between devices: none -> 20.1 us  [the longest x3 16.1 us: to_heads(): lax.all_to_all(split, 'view', split_axis=0, concat_axis=0, tiled=True)]
    all_to_all x0 -> x1, blocking collectives: none -> 11.7 us  [shards(): lax.all_to_all(result.reshape(heads, count, -1), 'view', split_axis=0, co...]
    all_to_all x0 -> x4, waiting for transfers between devices: none -> 11.2 us  [the longest x3 9.7 us: to_heads(): lax.all_to_all(split, 'view', split_axis=0, concat_axis=0, tiled=True)]
  transfers between devices with their start and end apart: 9 -> 4, of which waited for: 9 -> 3; matrix products, arithmetic and copies ran while one was open for 4% -> 21% of each run, Pallas kernels for 0% -> 0%
where the time goes in v1:
time: 98.3 us; the launch traced here: 97.6 us
  matrix products  35.2 us (36%)
  starting transfers between devices  20.1 us (20%)
  local copies, waits for them, and re-layouts  15.5 us (16%)
  blocking collectives  11.7 us (12%)
  waiting for transfers between devices  11.2 us (11%)
  other arithmetic  3.46 us (4%)
    dot_general x8, matrix products, fast_dot(): return jnp.einsum(spec, left, right, preferred_element_type=jnp.float32)  27.8 us
    all_to_all x3, starting transfers between devices, to_heads(): lax.all_to_all(split, 'view', split_axis=0, concat_axis=0, tiled=True)  16.1 us
    all_to_all x1, blocking collectives, shards(): lax.all_to_all(result.reshape(heads, count, -1), 'view', split_axis=0, co...  11.7 us
    all_to_all x3, waiting for transfers between devices, to_heads(): lax.all_to_all(split, 'view', split_axis=0, concat_axis=0, tiled=True)  9.7 us
    unnamed x17, local copies, waits for them, and re-layouts  9.43 us
    dot_general x18, matrix products, exact_dot(): jnp.einsum('mij,mjk->mik', left, right, precision=lax.Precision.HIGHEST)  6.45 us
    all_to_all x1, starting transfers between devices, shards(): lax.all_to_all(stacked, 'view', split_axis=1, concat_axis=3, tiled=True)  4 us
  transfers between devices with their start and end apart: 4, of which 3 were waited for; matrix products, arithmetic and copies ran while one was open for 21% of the time, Pallas kernels for 0%

profile of v1, /device:TPU:1, one launch (start us, length us, event | category | flops | bytes accessed | tf_op | source)
XLA Modules:
  0.0 97.6 jit_solution(15641253426255701737)
XLA Ops:
  0.0 1.1 %copy.84 = bf16[64,1024]{0,1:T(8,128)(2,1)S(1)} copy(bf16[64,1024]{1,0:T(8,128)(2,1)} %param.11) | data formatting | bytes 262144 | tf_op args[3]
  1.1 0.9 reshape.92
  2.0 7.3 %all-to-all-start.3 = ((bf16[16,2,2048]{2,1,0:T(2,128)(2,1)}), bf16[16,2,2048]{2,1,0:T(2,128)(2,1)S(1)}, u32[]{:S(2)}, u32[]{:S(2)}) async-start(bf16[16,2,2048]{2,1,0:T(2,128)(2,1)} %reshape.92), calls=%async_computation.3 | async-start | bytes 262144 | tf_op jit(solution)/shard_map/all_to_all | solution.py:75
  9.3 1.4 %fusion.64 = bf16[16,3,64,64]{3,2,1,0:T(8,128)(2,1)S(1)} fusion(bf16[1,16,64,64]{3,2,0,1:T(8,128)(2,1)} %bitcast.224, bf16[2,16,64,64]{3,2,1,0:T(8,128)(2,1)} %param.12), kind=kLoop, calls=%fused_computation.95 | loop fusion | flops 786432 | bytes 786432
  10.7 1.3 %reshape.94 = bf16[16,2,6144]{2,1,0:T(2,128)(2,1)} reshape(bf16[16,3,64,64]{3,2,1,0:T(8,128)(2,1)S(1)} %fusion.64) | data formatting | bytes 786432
  12.0 3.5 %all-to-all-done.3 = bf16[16,2,2048]{2,1,0:T(2,128)(2,1)S(1)} async-done(((bf16[16,2,2048]{2,1,0:T(2,128)(2,1)}), bf16[16,2,2048]{2,1,0:T(2,128)(2,1)S(1)}, u32[]{:S(2)}, u32[]{:S(2)}) %all-to-all-start.3) | async-done | bytes 131104 | tf_op jit(solution)/shard_map/all_to_all | solution.py:75
  15.5 4.0 %all-to-all-start = ((bf16[16,2,6144]{2,1,0:T(2,128)(2,1)}), bf16[16,2,6144]{2,1,0:T(2,128)(2,1)S(1)}, u32[]{:S(2)}, u32[]{:S(2)}) async-start(bf16[16,2,6144]{2,1,0:T(2,128)(2,1)} %reshape.94), calls=%async_computation | async-start | bytes 786432 | tf_op jit(solution)/shard_map/all_to_all | solution.py:85
  19.5 1.8 %copy.78 = bf16[128,1024]{0,1:T(8,128)(2,1)} copy(bf16[128,1024]{1,0:T(8,128)(2,1)} %param.8) | data formatting | bytes 524288 | tf_op args[0]
  21.3 1.1 %copy.74 = bf16[128,1024]{0,1:T(8,128)(2,1)S(1)} copy(bf16[128,1024]{1,0:T(8,128)(2,1)} %param.9) | data formatting | bytes 524288 | tf_op args[1]
  22.4 0.7 convert_element_type.42
  23.1 0.8 reshape.87
  23.8 1.2 %dynamic_slice.6 = f32[1]{0:T(128)} dynamic-slice(f32[16]{0:T(128)} %param.14, s32[]{:T(128)S(6)} %select_n.9), dynamic_slice_sizes={1} | dynamic-slice | bytes 12 | tf_op jit(solution)/shard_map/dynamic_slice | solution.py:93
  25.1 0.8 fusion.34
  25.9 0.2 reshape.93
  26.1 0.2 copy.85
  26.3 0.2 reshape.86
  26.5 1.5 %all-to-all-done = bf16[16,2,6144]{2,1,0:T(2,128)(2,1)S(1)} async-done(((bf16[16,2,6144]{2,1,0:T(2,128)(2,1)}), bf16[16,2,6144]{2,1,0:T(2,128)(2,1)S(1)}, u32[]{:S(2)}, u32[]{:S(2)}) %all-to-all-start) | async-done | bytes 393248 | tf_op jit(solution)/shard_map/all_to_all | solution.py:85
  27.9 4.5 %all-to-all-start.2 = ((bf16[16,128,64]{1,2,0:T(8,128)(2,1)}), bf16[16,128,64]{1,2,0:T(8,128)(2,1)S(1)}, u32[]{:S(2)}, u32[]{:S(2)}) async-start(bf16[16,128,64]{1,2,0:T(8,128)(2,1)} %bitcast.8), calls=%async_computation.2 | async-start | bytes 524288 | tf_op jit(solution)/shard_map/all_to_all | solution.py:75
  32.4 0.5 reshape.95
  33.0 0.2 copy.81
  33.2 0.2 squeeze.25
  33.4 6.2 %all-to-all-done.2 = bf16[16,128,64]{1,2,0:T(8,128)(2,1)S(1)} async-done(((bf16[16,128,64]{1,2,0:T(8,128)(2,1)}), bf16[16,128,64]{1,2,0:T(8,128)(2,1)S(1)}, u32[]{:S(2)}, u32[]{:S(2)}) %all-to-all-start.2) | async-done | bytes 262176 | tf_op jit(solution)/shard_map/all_to_all | solution.py:75
  39.6 4.3 %all-to-all-start.1 = ((bf16[16,128,64]{1,2,0:T(8,128)(2,1)}), bf16[16,128,64]{1,2,0:T(8,128)(2,1)S(1)}, u32[]{:S(2)}, u32[]{:S(2)}) async-start(bf16[16,128,64]{1,2,0:T(8,128)(2,1)} %fusion.34), calls=%async_computation.1 | async-start | bytes 524288 | tf_op jit(solution)/shard_map/all_to_all | solution.py:75
  44.0 4.5 %fusion.40 = f32[1024,2048]{0,1:T(8,128)} fusion(bf16[64,1024]{1,0:T(8,128)(2,1)S(1)} %squeeze.25, bf16[16,128,64]{1,2,0:T(8,128)(2,1)S(1)} %all-to-all-done.2), kind=kOutput, calls=%fused_computation.56 | convolution fusion | flops 268435456 | bytes 8781824 | tf_op jit(solution)/shard_map/td,df->tf/dot_general | solution.py:19
  48.5 0.2 copy.77
  48.7 0.2 squeeze.24
  48.9 0.2 copy.76
  49.1 0.2 squeeze.23
  49.3 4.5 %fusion.42 = f32[1024,2048]{0,1:T(8,128)} fusion(bf16[64,1024]{1,0:T(8,128)(2,1)S(1)} %squeeze.24, bf16[16,128,64]{1,2,0:T(8,128)(2,1)S(1)} %all-to-all-done.2), kind=kOutput, calls=%fused_computation.58 | convolution fusion | flops 268435456 | bytes 8781824 | tf_op jit(solution)/shard_map/td,df->tf/dot_general | solution.py:19
  53.8 1.3 %fusion.36 = f32[2048,1024]{1,0:T(8,128)S(1)} fusion(bf16[64,1024]{1,0:T(8,128)(2,1)S(1)} %squeeze.23, bf16[16,128,64]{1,2,0:T(8,128)(2,1)S(1)} %all-to-all-done.1), kind=kOutput, calls=%fused_computation.52 | convolution fusion | flops 268435456 | bytes 8781824 | tf_op jit(solution)/shard_map/td,df->tf/dot_general | solution.py:19
  55.1 2.1 %copy-done = f32[1024,2048]{0,1:T(8,128)S(1)} copy-done((f32[1024,2048]{0,1:T(8,128)S(1)}, f32[1024,2048]{0,1:T(8,128)}, u32[]{:S(2)}) %copy-start) | copy-done | bytes 8388632
  57.2 5.1 %fusion.22 = f32[1,64,1024]{2,1,0:T(8,128)S(1)} fusion(f32[1024,2048]{0,1:T(8,128)S(1)} %copy-done, f32[1024,2048]{0,1:T(8,128)} %fusion.40, bf16[16,128,64]{1,2,0:T(8,128)(2,1)S(1)} %all-to-all-done.1), kind=kOutput, calls=%fused_computation.29 | convolution fusion | flops 281018368 | bytes 17301504 | tf_op jit(solution)/shard_map/td,tf->df/dot_general | solution.py:19
  62.3 3.3 %fusion.19 = f32[1,64,1024]{2,1,0:T(8,128)S(1)} fusion(f32[1024,2048]{0,1:T(8,128)S(1)} %bitcast.218, f32[2048,1024]{1,0:T(8,128)S(1)} %fusion.36, f32[1024,2048]{0,1:T(8,128)S(1)} %copy-done, bf16[16,128,64]{1,2,0:T(8,128)(2,1)S(1)} %all-to-all-done.2), kind=kOutput, calls=%fused_computation.28 | convolution fusion | flops 289406976 | bytes 25690112 | tf_op jit(solution)/shard_map/td,tf->df/dot_general | solution.py:19
  65.6 2.4 %fusion.25 = f32[1,64,1024]{2,1,0:T(8,128)S(1)} fusion(f32[2048,1024]{1,0:T(8,128)S(1)} %fusion.36, f32[1024,2048]{0,1:T(8,128)S(1)} %bitcast.218, bf16[16,128,64]{1,2,0:T(8,128)(2,1)S(1)} %all-to-all-done.2), kind=kOutput, calls=%fused_computation.30 | convolution fusion | flops 281018368 | bytes 17301504 | tf_op jit(solution)/shard_map/td,tf->df/dot_general | solution.py:19
  68.1 0.9 select_reduce_fusion
  69.0 0.3 fusion.26
  69.3 0.3 fusion.52
  69.6 0.2 fusion.65
  69.8 0.2 fusion.27
  70.1 0.2 fusion.72
  70.3 0.2 fusion.66
  70.5 0.2 bitcast_convert_fusion
  70.7 0.3 multiply_reduce_fusion
  71.0 0.2 fusion.67
  71.2 0.2 fusion.28
  71.4 0.2 fusion.68
  71.7 0.2 fusion.73
  71.9 0.2 fusion.69
  72.1 0.2 fusion.29
  72.4 0.2 fusion.70
  72.6 0.2 fusion.74
  72.9 0.2 fusion.71
  73.1 0.2 fusion.30
  73.3 0.9 copy.73
  74.2 0.4 reshape.90
  74.8 0.2 convolution_multiply_fusion.1
  75.0 2.5 %multiply_reduce_fusion.1 = (f32[3,1024]{1,0:T(4,128)S(1)}, f32[3,64,1024]{2,1,0:T(8,128)S(1)}) fusion(f32[3,64,1024]{2,1,0:T(8,128)S(1)} %reshape.90, f32[3,64,64]{2,1,0:T(8,128)S(1)} %convolution_multiply_fusion.1, f32[1,64,1024]{2,1,0:T(8,128)S(1)} %fusion.22, f32[1,64,1024]{2,1,0:T(8,128)} %copy-done.1, f32[1,64,1024]{2,1,0:T(8,128)S(1)} %fusion.19, ...), kind=kOutput, calls=%fused_computation.45 | convolution fusion | flops 152171520 | bytes 2420740 | tf_op jit(solution)/shard_map/mij,mjk->mik/dot_general | solution.py:15
  77.6 2.9 %fusion.50 = f32[1024,1024]{1,0:T(8,128)} fusion(bf16[1024,64]{0,1:T(8,128)(2,1)S(1)} %reshape.86, bf16[3,64,1024]{2,1,0:T(8,128)(2,1)S(1)} %multiply_convert_fusion.4), kind=kOutput, calls=%fused_computation.70 | convolution fusion | flops 134217728 | bytes 4456448 | tf_op jit(solution)/shard_map/td,df->tf/dot_general | solution.py:19
  80.5 3.7 %multiply_reduce_fusion.2 = (f32[1024]{0:T(1024)S(1)}, f32[1024,64]{0,1:T(8,128)S(1)}) fusion(f32[1024,1024]{1,0:T(8,128)} %fusion.50, bf16[1024,64]{0,1:T(8,128)(2,1)S(1)} %reshape.86, bf16[3,64,1024]{2,1,0:T(8,128)(2,1)S(1)} %multiply_convert_fusion.4), kind=kOutput, calls=%fused_computation.61 | convolution fusion | flops 274856960 | bytes 4853760 | tf_op jit(solution)/shard_map/tf,df->td/dot_general | solution.py:19
  84.4 0.2 reshape.88
  84.6 0.2 reshape.96
  84.9 11.7 %all_to_all.35 = bf16[16,2,2048]{2,1,0:T(2,128)(2,1)S(1)} all-to-all(bf16[16,2,2048]{2,1,0:T(2,128)(2,1)S(1)} %reshape.96), channel_id=1, replica_groups=mesh['scene'=16,'view'=16] {'view'}, dimensions={0} | all-to-all | bytes 262144 | tf_op jit(solution)/shard_map/all_to_all | solution.py:97
  96.6 0.2 reshape.97
  96.8 0.8 copy.87
  (22 shorter events, 0.5 us)
Async XLA Ops:
  2.0 13.5 %all-to-all-start.3 = ((bf16[16,2,2048]{2,1,0:T(2,128)(2,1)}), bf16[16,2,2048]{2,1,0:T(2,128)(2,1)S(1)}, u32[]{:S(2)}, u32[]{:S(2)}) async-start(bf16[16,2,2048]{2,1,0:T(2,128)(2,1)} %reshape.92), calls=%async_computation.3 | async-start | bytes 262144 | tf_op jit(solution)/shard_map/all_to_all | solution.py:75
  15.5 12.5 %all-to-all-start = ((bf16[16,2,6144]{2,1,0:T(2,128)(2,1)}), bf16[16,2,6144]{2,1,0:T(2,128)(2,1)S(1)}, u32[]{:S(2)}, u32[]{:S(2)}) async-start(bf16[16,2,6144]{2,1,0:T(2,128)(2,1)} %reshape.94), calls=%async_computation | async-start | bytes 786432 | tf_op jit(solution)/shard_map/all_to_all | solution.py:85
  27.9 11.7 %all-to-all-start.2 = ((bf16[16,128,64]{1,2,0:T(8,128)(2,1)}), bf16[16,128,64]{1,2,0:T(8,128)(2,1)S(1)}, u32[]{:S(2)}, u32[]{:S(2)}) async-start(bf16[16,128,64]{1,2,0:T(8,128)(2,1)} %bitcast.8), calls=%async_computation.2 | async-start | bytes 524288 | tf_op jit(solution)/shard_map/all_to_all | solution.py:75
  39.6 14.1 %all-to-all-start.1 = ((bf16[16,128,64]{1,2,0:T(8,128)(2,1)}), bf16[16,128,64]{1,2,0:T(8,128)(2,1)S(1)}, u32[]{:S(2)}, u32[]{:S(2)}) async-start(bf16[16,128,64]{1,2,0:T(8,128)(2,1)} %fusion.34), calls=%async_computation.1 | async-start | bytes 524288 | tf_op jit(solution)/shard_map/all_to_all | solution.py:75
  53.8 3.4 %copy-start = (f32[1024,2048]{0,1:T(8,128)S(1)}, f32[1024,2048]{0,1:T(8,128)}, u32[]{:S(2)}) copy-start(f32[1024,2048]{0,1:T(8,128)} %fusion.42) | copy-start | bytes 25165828
  53.8 8.5 %slice-start = ((s8[8388608]{0:T(1024)(128)(4,1)}), s8[4194304]{0:T(1024)(128)(4,1)S(1)}, s32[]{:S(2)}) async-start(s8[8388608]{0:T(1024)(128)(4,1)} %bitcast.217), calls=%async_computation.5 | async-start | bytes 8388608
  57.2 5.1 %slice-start.1 = ((s8[8388608]{0:T(1024)(128)(4,1)}), s8[4194304]{0:T(1024)(128)(4,1)S(1)}, s32[]{:S(2)}) async-start(s8[8388608]{0:T(1024)(128)(4,1)} %bitcast.217), calls=%async_computation.6 | async-start | bytes 8388608
  68.0 4.8 %copy-start.1 = (f32[1,64,1024]{2,1,0:T(8,128)}, f32[1,64,1024]{2,1,0:T(8,128)S(1)}, u32[]{:S(2)}) copy-start(f32[1,64,1024]{2,1,0:T(8,128)S(1)} %fusion.25) | copy-start | bytes 786436

commit v2 on v1

v2 whole, which is shorter than its diff:
```python
import jax
import jax.numpy as jnp
from jax import lax
from jax.experimental import pallas as pl
from jax.experimental.pallas import tpu as pltpu
from jax.sharding import PartitionSpec as P

NS_STEPS = 5
GROUP = 16
DH = 64
HID = 1024
LANES = 128
BLOCK = 128

poly_one = 3.4445
poly_two = -4.775
poly_three = 2.0315

ROWS_BY_ROWS = (((1,), (1,)), ((), ()))
COLS_BY_COLS = (((0,), (0,)), ((), ()))


def nt_dot(left, right):
    return lax.dot_general(left, right, ROWS_BY_ROWS, preferred_element_type=jnp.float32)


def plain_dot(left, right):
    return jnp.dot(left, right, preferred_element_type=jnp.float32)


def exact_dot(left, right):
    return jnp.dot(
        left, right, precision=lax.Precision.HIGHEST, preferred_element_type=jnp.float32
    )


def flip(block):
    return block.T


def clear_grads(grad):
    grad[...] = jnp.zeros_like(grad)


def unpack_weights(source, recv_w, weight, query):
    turned = flip(recv_w[source])
    low = pl.ds(pl.multiple_of(source * DH, DH), DH)
    weight[0, low, :] = turned[:DH, :DH]
    weight[1, low, :] = turned[:DH, DH:]
    weight[2, low, :] = turned[DH:, :DH]
    query[low, :] = turned[DH:, DH:]


def grad_chunk(pair, recv_t, weight, grad):
    key_cols = recv_t[pair, :DH, :]
    err_cols = recv_t[pair, DH:, :]

    def one(at):
        rows = pl.ds(pl.multiple_of(at * BLOCK, BLOCK), BLOCK)
        gate = plain_dot(weight[0, rows, :], key_cols)
        up = plain_dot(weight[1, rows, :], key_cols)
        back = plain_dot(weight[2, rows, :], err_cols)
        sigma = 0.5 * jnp.tanh(0.5 * gate) + 0.5
        gated = gate * sigma
        hidden = (gated * up).astype(jnp.bfloat16)
        up_term = (back * gated).astype(jnp.bfloat16)
        gate_term = (back * up * (sigma + gated * (1.0 - sigma))).astype(jnp.bfloat16)
        grad[0, rows, :] += nt_dot(gate_term, key_cols)
        grad[1, rows, :] += nt_dot(up_term, key_cols)
        grad[2, rows, :] += nt_dot(hidden, err_cols)

    def loop_body(at, carry):
        one(at)
        return carry

    lax.fori_loop(0, HID // BLOCK, loop_body, 0, unroll=True)


def orthogonalizers(grad):
    grams, totals = [], []
    eye = (
        lax.broadcasted_iota(jnp.int32, (DH, DH), 0) == lax.broadcasted_iota(jnp.int32, (DH, DH), 1)
    ).astype(jnp.float32)
    for part in range(3):
        gram = lax.dot_general(
            grad[part],
            grad[part],
            COLS_BY_COLS,
            precision=lax.Precision.HIGHEST,
            preferred_element_type=jnp.float32,
        )
        square_norm = jnp.sum(gram * eye, axis=(0, 1), keepdims=True)
        factor = 1.0 / (jnp.sqrt(square_norm) + 1e-07)
        grams.append(gram * (factor * factor))
        totals.append(factor * eye)
    for step in range(NS_STEPS):
        squares = [exact_dot(gram, gram) for gram in grams]
        blends = [
            poly_one * eye + poly_two * gram + poly_three * square
            for gram, square in zip(grams, squares)
        ]
        totals = [
            blend * total[:1, :1] if step == 0 else exact_dot(blend, total)
            for blend, total in zip(blends, totals)
        ]
        if step < NS_STEPS - 1:
            cubes = [exact_dot(gram, square) for gram, square in zip(grams, squares)]
            halves = [
                poly_one * gram + poly_two * square + poly_three * cube
                for gram, square, cube in zip(grams, squares, cubes)
            ]
            grams = [exact_dot(half, blend) for half, blend in zip(halves, blends)]
    return totals


def renew(grad, weight, fresh, step_size):
    totals = orthogonalizers(grad)
    for part in range(3):
        start = weight[part].astype(jnp.float32)
        moved = start - step_size * exact_dot(grad[part], totals[part])
        keep = jnp.sum(start * start, axis=1, keepdims=True)
        length = jnp.sum(moved * moved, axis=1, keepdims=True)
        fresh[part] = (moved * (jnp.sqrt(keep) / (jnp.sqrt(length) + 1e-06))).astype(jnp.bfloat16)


QROWS = 256


def apply_block(at, query, fresh, gain, send_o):
    rows = pl.ds(pl.multiple_of(at * QROWS, QROWS), QROWS)
    block = query[rows, :]
    hidden = []
    for half in range(4):
        cols = pl.ds(half * 256, 256)
        gate = nt_dot(block, fresh[0, cols, :])
        up = nt_dot(block, fresh[1, cols, :])
        sigma = 0.5 * jnp.tanh(0.5 * gate) + 0.5
        hidden.append((gate * sigma * up).astype(jnp.bfloat16))
    head_out = plain_dot(jnp.concatenate(hidden, axis=1), fresh[2])
    mean_square = jnp.sum(head_out * head_out, axis=1, keepdims=True) * (1.0 / DH)
    done = head_out * lax.rsqrt(mean_square + 1e-06) * gain
    for piece in range(QROWS // DH):
        top = done[piece * DH : piece * DH + DH // 2]
        bottom = done[piece * DH + DH // 2 : (piece + 1) * DH]
        send_o[at * (QROWS // DH) + piece] = jnp.concatenate([top, bottom], axis=1).astype(
            jnp.bfloat16
        )


def turn_tokens(pair, keys, values, rate_rows, queries, turned_q, send_t):
    cols = pl.ds(pl.multiple_of(pair * LANES, LANES), LANES)
    turned_k = flip(keys[:, cols])
    turned_v = flip(values[:, cols]).astype(jnp.float32)
    for side in range(2):
        head = 2 * pair + side
        rate = rate_rows[pl.ds(head, 1), :]
        part = slice(side * DH, (side + 1) * DH)
        send_t[head, :DH, :] = turned_k[part]
        send_t[head, DH:, :] = (-(rate * turned_v[part])).astype(jnp.bfloat16)


def pack_weights(pair, queries, gate_up, down_t, send_w):
    cols = pl.ds(pl.multiple_of(pair * LANES, LANES), LANES)
    turned_q = flip(queries[:, cols])
    for side in range(2):
        head = 2 * pair + side
        send_w[head, :DH, :] = jnp.concatenate([gate_up[0, head], down_t[head]], axis=1)
        send_w[head, DH:, :] = jnp.concatenate(
            [gate_up[1, head], turned_q[side * DH : (side + 1) * DH]], axis=1
        )


def whole_kernel(
    keys,
    values,
    rates,
    queries,
    gate_up,
    down_t,
    step_sizes,
    gain_rows,
    outputs,
    send_w,
    recv_w,
    send_t,
    recv_t,
    send_o,
    recv_o,
    rate_rows,
    weight,
    query,
    grad,
    fresh,
    w_out,
    w_in,
    t_out,
    t_in,
    o_out,
    o_in,
    here,
):
    me = lax.axis_index("view")
    my_pair, my_side = me // 2, me % 2
    my_cols = pl.ds(pl.multiple_of(my_side * LANES, LANES), LANES)

    def peer(step):
        return lax.rem(me + step, GROUP)

    def loop(count, one, first=0):
        def loop_body(at, carry):
            one(at)
            return carry

        lax.fori_loop(first, count, loop_body, 0)

    barrier = pltpu.get_barrier_semaphore()

    def greet(step):
        pl.semaphore_signal(
            barrier,
            inc=1,
            device_id={"view": peer(step)},
            device_id_type=pl.DeviceIdType.MESH,
        )

    loop(GROUP, greet, 1)

    def w_copy(target, origin):
        return pltpu.make_async_remote_copy(
            src_ref=send_w.at[target],
            dst_ref=recv_w.at[origin],
            send_sem=w_out.at[target],
            recv_sem=w_in.at[origin],
            device_id={"view": target},
            device_id_type=pl.DeviceIdType.MESH,
        )

    def t_copy(target, origin):
        cols = pl.ds(pl.multiple_of(lax.rem(origin, 2) * LANES, LANES), LANES)
        return pltpu.make_async_remote_copy(
            src_ref=send_t.at[target],
            dst_ref=recv_t.at[lax.div(origin, 2), :, cols],
            send_sem=t_out.at[target],
            recv_sem=t_in.at[origin],
            device_id={"view": target},
            device_id_type=pl.DeviceIdType.MESH,
        )

    def o_copy(target, origin):
        return pltpu.make_async_remote_copy(
            src_ref=send_o.at[target],
            dst_ref=recv_o.at[origin],
            send_sem=o_out.at[target],
            recv_sem=o_in.at[origin],
            device_id={"view": target},
            device_id_type=pl.DeviceIdType.MESH,
        )

    loop(GROUP // 2, lambda pair: pack_weights(pair, queries, gate_up, down_t, send_w))
    pl.semaphore_wait(barrier, GROUP - 1)

    loop(GROUP, lambda step: w_copy(peer(step), me).start(), 1)
    rate_rows[...] = flip(rates[...].astype(jnp.float32))
    loop(
        GROUP // 2,
        lambda pair: turn_tokens(pair, keys, values, rate_rows, None, None, send_t),
    )
    loop(GROUP, lambda step: t_copy(peer(step), me).start(), 1)

    own_w = pltpu.make_async_copy(send_w.at[me], recv_w.at[me], here.at[0])
    own_t = pltpu.make_async_copy(send_t.at[me], recv_t.at[my_pair, :, my_cols], here.at[1])
    own_w.start()
    own_t.start()
    clear_grads(grad)
    own_w.wait()
    unpack_weights(me, recv_w, weight, query)

    def take_weights(step):
        origin = peer(GROUP - step)
        w_copy(origin, origin).wait_recv()
        unpack_weights(origin, recv_w, weight, query)

    loop(GROUP, take_weights, 1)
    own_t.wait()
    other = my_pair * 2 + 1 - my_side
    t_copy(other, other).wait_recv()
    grad_chunk(my_pair, recv_t, weight, grad)

    def take_tokens(step):
        pair = lax.rem(my_pair + GROUP // 2 - step, GROUP // 2)
        t_copy(2 * pair, 2 * pair).wait_recv()
        t_copy(2 * pair + 1, 2 * pair + 1).wait_recv()
        grad_chunk(pair, recv_t, weight, grad)

    loop(GROUP // 2, take_tokens, 1)

    renew(grad, weight, fresh, step_sizes[me])
    gain = gain_rows[pl.ds(my_pair, 1), :]
    gain = jnp.where(my_side == 0, gain[:, :DH], gain[:, DH:])

    for at in range(HID // QROWS):
        apply_block(at, query, fresh, gain, send_o)
        for target in range(at * (QROWS // DH), (at + 1) * (QROWS // DH)):

            @pl.when(target != me)
            def _():
                o_copy(target, me).start()

    own_o = pltpu.make_async_copy(send_o.at[me], recv_o.at[me], here.at[2])
    own_o.start()
    own_o.wait()

    def take_outputs(step):
        o_copy(peer(step), peer(step)).wait_recv()

    loop(GROUP, take_outputs, 1)
    for pair in range(GROUP // 2):
        even, odd = recv_o[2 * pair], recv_o[2 * pair + 1]
        cols = slice(pair * LANES, (pair + 1) * LANES)
        outputs[: DH // 2, cols] = jnp.concatenate([even[:, :DH], odd[:, :DH]], axis=1)
        outputs[DH // 2 :, cols] = jnp.concatenate([even[:, DH:], odd[:, DH:]], axis=1)

    def finish_sends(step):
        w_copy(peer(step), me).wait_send()
        t_copy(peer(step), me).wait_send()
        o_copy(peer(step), me).wait_send()

    loop(GROUP, finish_sends, 1)


def shards(keys, values, rates, queries, gate_up, down_t, step_sizes, gain):
    vmem = pl.BlockSpec(memory_space=pltpu.VMEM)
    smem = pl.BlockSpec(memory_space=pltpu.SMEM)
    bf16, f32 = jnp.bfloat16, jnp.float32
    sems = pltpu.SemaphoreType.DMA((GROUP,))
    return pl.pallas_call(
        whole_kernel,
        out_shape=jax.ShapeDtypeStruct(queries.shape, bf16),
        in_specs=[vmem] * 6 + [smem, vmem],
        out_specs=vmem,
        scratch_shapes=[
            pltpu.VMEM((GROUP, 2 * DH, LANES), bf16),
            pltpu.VMEM((GROUP, 2 * DH, LANES), bf16),
            pltpu.VMEM((GROUP, 2 * DH, LANES), bf16),
            pltpu.VMEM((GROUP // 2, 2 * DH, 2 * LANES), bf16),
            pltpu.VMEM((GROUP, DH // 2, LANES), bf16),
            pltpu.VMEM((GROUP, DH // 2, LANES), bf16),
            pltpu.VMEM((GROUP, LANES), f32),
            pltpu.VMEM((3, HID, DH), bf16),
            pltpu.VMEM((HID, DH), bf16),
            pltpu.VMEM((3, HID, DH), f32),
            pltpu.VMEM((3, HID, DH), bf16),
        ]
        + [sems] * 6
        + [pltpu.SemaphoreType.DMA((3,))],
        compiler_params=pltpu.CompilerParams(
            collective_id=0, has_side_effects=True, vmem_limit_bytes=48 << 20
        ),
    )(keys, values, rates, queries, gate_up, down_t, step_sizes, gain.reshape(GROUP // 2, LANES))


def solution(mesh):
    return jax.shard_map(
        shards,
        mesh=mesh,
        in_specs=(
            P(("scene", "view"), None),
            P(("scene", "view"), None),
            P(("scene", "view"), None),
            P(("scene", "view"), None),
            P(None, None, None, "view"),
            P(None, None, "view"),
            P(),
            P(),
        ),
        out_specs=P(("scene", "view"), None),
        check_vma=False,
    )
```

time: 98.3 us -> 48.8 us (0.50)
  Pallas kernels: 0 us -> 42.2 us
  matrix products: 35.2 us -> 0 us
  starting transfers between devices: 20.1 us -> 0 us
  blocking collectives: 11.7 us -> 0 us
  waiting for transfers between devices: 11.2 us -> 0 us
  local copies, waits for them, and re-layouts: 15.5 us -> 6.28 us
  other arithmetic: 3.46 us -> 0 us
    pallas_call x0 -> x1, Pallas kernels: none -> 42.2 us  [shards(): pl.pallas_call(whole_kernel, out_shape=jax.ShapeDtypeStruct(queries.shape...]
    dot_general x27 -> x0, matrix products: 35.2 us -> none  [the longest x8 27.8 us: fast_dot(): return jnp.einsum(spec, left, right, preferred_element_type=jnp.float32)]
    all_to_all x4 -> x0, starting transfers between devices: 20.1 us -> none  [the longest x3 16.1 us: to_heads(): lax.all_to_all(split, 'view', split_axis=0, concat_axis=0, tiled=True)]
    all_to_all x1 -> x0, blocking collectives: 11.7 us -> none  [shards(): lax.all_to_all(result.reshape(heads, count, -1), 'view', split_axis=0, co...]
    all_to_all x4 -> x0, waiting for transfers between devices: 11.2 us -> none  [the longest x3 9.7 us: to_heads(): lax.all_to_all(split, 'view', split_axis=0, concat_axis=0, tiled=True)]
    unnamed x17 -> x16, local copies, waits for them, and re-layouts: 9.43 us -> 6.28 us
    reshape x5 -> x0, local copies, waits for them, and re-layouts: 1.99 us -> none  [the longest x1 0.79 us: shards(): return back.transpose(1, 0, 2).reshape(count, -1)]
    convert_element_type x2 -> x0, local copies, waits for them, and re-layouts: 1.36 us -> none  [renew_weights(): weights = stacked.astype(jnp.float32)]
  transfers between devices with their start and end apart: 4 -> 0, of which waited for: 3 -> 0; matrix products, arithmetic and copies ran while one was open for 21% -> 0% of each run, Pallas kernels for 0% -> 0%
where the time goes in v2:
time: 48.8 us; the launch traced here: 48.5 us
  Pallas kernels  42.2 us (86%)
  local copies, waits for them, and re-layouts  6.28 us (13%)
    pallas_call x1, Pallas kernels, shards(): pl.pallas_call(whole_kernel, out_shape=jax.ShapeDtypeStruct(queries.shape...  42.2 us
    unnamed x16, local copies, waits for them, and re-layouts  6.28 us

profile of v2, /device:TPU:1, one launch (start us, length us, event | category | flops | bytes accessed | tf_op | source)
XLA Modules:
  0.0 48.5 jit_solution(4695850202478941351)
XLA Ops:
  0.0 0.0 copy-start.5
  0.0 0.0 copy-start.6
  0.0 0.8 %copy.9.rates = bf16[128,16]{1,0:T(8,128)(2,1)S(1)} copy(bf16[128,16]{0,1:T(8,128)(2,1)} %param.10) | data formatting | bytes 8192 | tf_op args[2]
  0.8 0.0 copy-done.5
  0.8 0.0 copy-done.6
  0.8 0.0 copy-start
  0.9 1.0 %copy-done = bf16[2,16,64,64]{3,2,1,0:T(8,128)(2,1)S(1)} copy-done((bf16[2,16,64,64]{3,2,1,0:T(8,128)(2,1)S(1)}, bf16[2,16,64,64]{3,2,1,0:T(8,128)(2,1)}, u32[]{:S(2)}) %copy-start) | copy-done | bytes 262168
  1.9 0.0 copy-start.1
  1.9 0.9 %copy-done.1 = bf16[128,1024]{1,0:T(8,128)(2,1)S(1)} copy-done((bf16[128,1024]{1,0:T(8,128)(2,1)S(1)}, bf16[128,1024]{1,0:T(8,128)(2,1)}, u32[]{:S(2)}) %copy-start.1) | copy-done | bytes 262168
  2.8 0.0 copy-start.2
  2.8 0.9 %copy-done.2 = bf16[128,1024]{1,0:T(8,128)(2,1)S(1)} copy-done((bf16[128,1024]{1,0:T(8,128)(2,1)S(1)}, bf16[128,1024]{1,0:T(8,128)(2,1)}, u32[]{:S(2)}) %copy-start.2) | copy-done | bytes 262168
  3.8 0.0 copy-start.3
  3.8 0.9 %copy-done.3 = bf16[16,64,64]{2,1,0:T(8,128)(2,1)S(1)} copy-done((bf16[16,64,64]{2,1,0:T(8,128)(2,1)S(1)}, bf16[16,64,64]{2,1,0:T(8,128)(2,1)}, u32[]{:S(2)}) %copy-start.3) | copy-done | bytes 131096
  4.7 0.0 copy-start.4
  4.7 0.9 %copy-done.4 = bf16[64,1024]{1,0:T(8,128)(2,1)S(1)} copy-done((bf16[64,1024]{1,0:T(8,128)(2,1)S(1)}, bf16[64,1024]{1,0:T(8,128)(2,1)}, u32[]{:S(2)}) %copy-start.4) | copy-done | bytes 131096
  5.6 42.2 %shard_map.82 = bf16[64,1024]{1,0:T(8,128)(2,1)S(1)} custom-call(bf16[128,1024]{1,0:T(8,128)(2,1)S(1)} %copy-done.1, bf16[128,1024]{1,0:T(8,128)(2,1)S(1)} %copy-done.2, bf16[128,16]{1,0:T(8,128)(2,1)S(1)} %copy.9.rates, bf16[64,1024]{1,0:T(8,128)(2,1)S(1)} %copy-done.4, bf16[2,16,64,64]{3,2,1,0:T(8,128)(2,1)S(1)} %copy-done, ...), custom_call_target="tpu_custom_call" | custom-call | tf_op jit(solution)/shard_map/pallas_call | solution.py:336
  47.9 0.7 %copy.11 = bf16[64,1024]{1,0:T(8,128)(2,1)} copy(bf16[64,1024]{1,0:T(8,128)(2,1)S(1)} %shard_map.82) | data formatting | bytes 262144
Async XLA Ops:
  0.0 0.8 %copy-start.5 = (f32[1024]{0:T(1024)S(1)}, f32[1024]{0:T(1024)}, u32[]{:S(2)}) copy-start(f32[1024]{0:T(1024)} %param.15) | copy-start | bytes 12292
  0.0 0.8 %copy-start.6 = (f32[16]{0:T(128)S(1)}, f32[16]{0:T(128)}, u32[]{:S(2)}) copy-start(f32[16]{0:T(128)} %step_sizes.1) | copy-start | bytes 196
  0.8 1.0 %copy-start = (bf16[2,16,64,64]{3,2,1,0:T(8,128)(2,1)S(1)}, bf16[2,16,64,64]{3,2,1,0:T(8,128)(2,1)}, u32[]{:S(2)}) copy-start(bf16[2,16,64,64]{3,2,1,0:T(8,128)(2,1)} %gate_up.1) | copy-start | bytes 786436
  1.9 0.9 %copy-start.1 = (bf16[128,1024]{1,0:T(8,128)(2,1)S(1)}, bf16[128,1024]{1,0:T(8,128)(2,1)}, u32[]{:S(2)}) copy-start(bf16[128,1024]{1,0:T(8,128)(2,1)} %keys.1) | copy-start | bytes 786436
  2.8 0.9 %copy-start.2 = (bf16[128,1024]{1,0:T(8,128)(2,1)S(1)}, bf16[128,1024]{1,0:T(8,128)(2,1)}, u32[]{:S(2)}) copy-start(bf16[128,1024]{1,0:T(8,128)(2,1)} %values.1) | copy-start | bytes 786436
  3.8 0.9 %copy-start.3 = (bf16[16,64,64]{2,1,0:T(8,128)(2,1)S(1)}, bf16[16,64,64]{2,1,0:T(8,128)(2,1)}, u32[]{:S(2)}) copy-start(bf16[16,64,64]{2,1,0:T(8,128)(2,1)} %down_t.1) | copy-start | bytes 393220
  4.7 0.9 %copy-start.4 = (bf16[64,1024]{1,0:T(8,128)(2,1)S(1)}, bf16[64,1024]{1,0:T(8,128)(2,1)}, u32[]{:S(2)}) copy-start(bf16[64,1024]{1,0:T(8,128)(2,1)} %queries.1) | copy-start | bytes 393220

commit v3 on v2

--- a/solution.py
+++ b/solution.py
@@ -10,7 +10,6 @@
 DH = 64
 HID = 1024
 LANES = 128
-BLOCK = 128
 
 poly_one = 3.4445
 poly_two = -4.775
@@ -55,25 +54,17 @@
     key_cols = recv_t[pair, :DH, :]
     err_cols = recv_t[pair, DH:, :]
 
-    def one(at):
-        rows = pl.ds(pl.multiple_of(at * BLOCK, BLOCK), BLOCK)
-        gate = plain_dot(weight[0, rows, :], key_cols)
-        up = plain_dot(weight[1, rows, :], key_cols)
-        back = plain_dot(weight[2, rows, :], err_cols)
-        sigma = 0.5 * jnp.tanh(0.5 * gate) + 0.5
-        gated = gate * sigma
-        hidden = (gated * up).astype(jnp.bfloat16)
-        up_term = (back * gated).astype(jnp.bfloat16)
-        gate_term = (back * up * (sigma + gated * (1.0 - sigma))).astype(jnp.bfloat16)
-        grad[0, rows, :] += nt_dot(gate_term, key_cols)
-        grad[1, rows, :] += nt_dot(up_term, key_cols)
-        grad[2, rows, :] += nt_dot(hidden, err_cols)
-
-    def loop_body(at, carry):
-        one(at)
-        return carry
-
-    lax.fori_loop(0, HID // BLOCK, loop_body, 0, unroll=True)
+    gate = plain_dot(weight[0], key_cols)
+    up = plain_dot(weight[1], key_cols)
+    back = plain_dot(weight[2], err_cols)
+    sigma = 0.5 * jnp.tanh(0.5 * gate) + 0.5
+    gated = gate * sigma
+    hidden = (gated * up).astype(jnp.bfloat16)
+    up_term = (back * gated).astype(jnp.bfloat16)
+    gate_term = (back * up * (sigma + gated * (1.0 - sigma))).astype(jnp.bfloat16)
+    grad[0] += nt_dot(gate_term, key_cols)
+    grad[1] += nt_dot(up_term, key_cols)
+    grad[2] += nt_dot(hidden, err_cols)
 
 
 def orthogonalizers(grad):
@@ -147,13 +138,15 @@
         )
 
 
-def turn_tokens(pair, keys, values, rate_rows, queries, turned_q, send_t):
+def turn_tokens(pair, keys, values, rates, send_t):
     cols = pl.ds(pl.multiple_of(pair * LANES, LANES), LANES)
     turned_k = flip(keys[:, cols])
     turned_v = flip(values[:, cols]).astype(jnp.float32)
+    pair_rates = rates[...].astype(jnp.float32)
+    row = lax.broadcasted_iota(jnp.int32, pair_rates.shape, 0)
     for side in range(2):
         head = 2 * pair + side
-        rate = rate_rows[pl.ds(head, 1), :]
+        rate = jnp.sum(jnp.where(row == head, pair_rates, 0.0), axis=0, keepdims=True)
         part = slice(side * DH, (side + 1) * DH)
         send_t[head, :DH, :] = turned_k[part]
         send_t[head, DH:, :] = (-(rate * turned_v[part])).astype(jnp.bfloat16)
@@ -171,6 +164,15 @@
 
 
 def whole_kernel(
+    keys_hbm,
+    values_hbm,
+    rates_hbm,
+    queries_hbm,
+    gate_up_hbm,
+    down_t_hbm,
+    steps_hbm,
+    gain_hbm,
+    outputs,
     keys,
     values,
     rates,
@@ -179,14 +181,12 @@
     down_t,
     step_sizes,
     gain_rows,
-    outputs,
     send_w,
     recv_w,
     send_t,
     recv_t,
     send_o,
     recv_o,
-    rate_rows,
     weight,
     query,
     grad,
@@ -198,7 +198,26 @@
     o_out,
     o_in,
     here,
+    loaded,
 ):
+    loads = [
+        pltpu.make_async_copy(far, near, loaded.at[at])
+        for at, (far, near) in enumerate(
+            (
+                (gate_up_hbm, gate_up),
+                (down_t_hbm, down_t),
+                (queries_hbm, queries),
+                (keys_hbm, keys),
+                (values_hbm, values),
+                (rates_hbm, rates),
+                (steps_hbm, step_sizes),
+                (gain_hbm, gain_rows),
+            )
+        )
+    ]
+    for load in loads:
+        load.start()
+
     me = lax.axis_index("view")
     my_pair, my_side = me // 2, me % 2
     my_cols = pl.ds(pl.multiple_of(my_side * LANES, LANES), LANES)
@@ -256,15 +275,15 @@
             device_id_type=pl.DeviceIdType.MESH,
         )
 
+    for load in loads[:3]:
+        load.wait()
     loop(GROUP // 2, lambda pair: pack_weights(pair, queries, gate_up, down_t, send_w))
     pl.semaphore_wait(barrier, GROUP - 1)
 
     loop(GROUP, lambda step: w_copy(peer(step), me).start(), 1)
-    rate_rows[...] = flip(rates[...].astype(jnp.float32))
-    loop(
-        GROUP // 2,
-        lambda pair: turn_tokens(pair, keys, values, rate_rows, None, None, send_t),
-    )
+    for load in loads[3:]:
+        load.wait()
+    loop(GROUP // 2, lambda pair: turn_tokens(pair, keys, values, rates, send_t))
     loop(GROUP, lambda step: t_copy(peer(step), me).start(), 1)
 
     own_w = pltpu.make_async_copy(send_w.at[me], recv_w.at[me], here.at[0])
@@ -329,34 +348,48 @@
 
 
 def shards(keys, values, rates, queries, gate_up, down_t, step_sizes, gain):
-    vmem = pl.BlockSpec(memory_space=pltpu.VMEM)
-    smem = pl.BlockSpec(memory_space=pltpu.SMEM)
     bf16, f32 = jnp.bfloat16, jnp.float32
     sems = pltpu.SemaphoreType.DMA((GROUP,))
     return pl.pallas_call(
         whole_kernel,
         out_shape=jax.ShapeDtypeStruct(queries.shape, bf16),
-        in_specs=[vmem] * 6 + [smem, vmem],
-        out_specs=vmem,
+        in_specs=[pl.BlockSpec(memory_space=pltpu.HBM)] * 8,
+        out_specs=pl.BlockSpec(memory_space=pltpu.VMEM),
         scratch_shapes=[
+            pltpu.VMEM(keys.shape, bf16),
+            pltpu.VMEM(values.shape, bf16),
+            pltpu.VMEM(rates.shape[::-1], bf16),
+            pltpu.VMEM(queries.shape, bf16),
+            pltpu.VMEM(gate_up.shape, bf16),
+            pltpu.VMEM(down_t.shape, bf16),
+            pltpu.SMEM(step_sizes.shape, f32),
+            pltpu.VMEM((GROUP // 2, LANES), f32),
             pltpu.VMEM((GROUP, 2 * DH, LANES), bf16),
             pltpu.VMEM((GROUP, 2 * DH, LANES), bf16),
             pltpu.VMEM((GROUP, 2 * DH, LANES), bf16),
             pltpu.VMEM((GROUP // 2, 2 * DH, 2 * LANES), bf16),
             pltpu.VMEM((GROUP, DH // 2, LANES), bf16),
             pltpu.VMEM((GROUP, DH // 2, LANES), bf16),
-            pltpu.VMEM((GROUP, LANES), f32),
             pltpu.VMEM((3, HID, DH), bf16),
             pltpu.VMEM((HID, DH), bf16),
             pltpu.VMEM((3, HID, DH), f32),
             pltpu.VMEM((3, HID, DH), bf16),
         ]
         + [sems] * 6
-        + [pltpu.SemaphoreType.DMA((3,))],
+        + [pltpu.SemaphoreType.DMA((3,)), pltpu.SemaphoreType.DMA((8,))],
         compiler_params=pltpu.CompilerParams(
             collective_id=0, has_side_effects=True, vmem_limit_bytes=48 << 20
         ),
-    )(keys, values, rates, queries, gate_up, down_t, step_sizes, gain.reshape(GROUP // 2, LANES))
+    )(
+        keys,
+        values,
+        rates.T,
+        queries,
+        gate_up,
+        down_t,
+        step_sizes,
+        gain.reshape(GROUP // 2, LANES),
+    )
 
 
 def solution(mesh):

time: 48.8 us -> 44.2 us (0.906)
  Pallas kernels: 42.2 us -> 36.4 us
  local copies, waits for them, and re-layouts: 6.28 us -> 7.48 us
    pallas_call x1, Pallas kernels: 42.2 us -> 36.4 us  [shards(): pl.pallas_call(whole_kernel, out_shape=jax.ShapeDtypeStruct(queries.shape...]
    unnamed x16 -> x17, local copies, waits for them, and re-layouts: 6.28 us -> 7.48 us
where the time goes in v3:
time: 44.2 us; the launch traced here: 43.9 us
  Pallas kernels  36.4 us (82%)
  local copies, waits for them, and re-layouts  7.48 us (17%)
    pallas_call x1, Pallas kernels, shards(): pl.pallas_call(whole_kernel, out_shape=jax.ShapeDtypeStruct(queries.shape...  36.4 us
    unnamed x17, local copies, waits for them, and re-layouts  7.48 us

profile of v3, /device:TPU:1, one launch (start us, length us, event | category | flops | bytes accessed | tf_op | source)
XLA Modules:
  0.0 43.9 jit_solution(17864169203049360036)
XLA Ops:
  0.0 0.0 copy-start.7
  0.0 0.7 %copy-done.7 = f32[16]{0:T(128)S(1)} copy-done((f32[16]{0:T(128)S(1)}, f32[16]{0:T(128)}, u32[]{:S(2)}) %copy-start.7) | copy-done | bytes 88
  0.7 0.0 copy-start
  0.7 1.0 %copy-done = bf16[2,16,64,64]{3,2,1,0:T(8,128)(2,1)S(1)} copy-done((bf16[2,16,64,64]{3,2,1,0:T(8,128)(2,1)S(1)}, bf16[2,16,64,64]{3,2,1,0:T(8,128)(2,1)}, u32[]{:S(2)}) %copy-start) | copy-done | bytes 262168
  1.7 0.0 copy-start.1
  1.7 0.9 %copy-done.1 = bf16[128,1024]{1,0:T(8,128)(2,1)S(1)} copy-done((bf16[128,1024]{1,0:T(8,128)(2,1)S(1)}, bf16[128,1024]{1,0:T(8,128)(2,1)}, u32[]{:S(2)}) %copy-start.1) | copy-done | bytes 262168
  2.6 0.0 copy-start.2
  2.7 0.9 %copy-done.2 = bf16[128,1024]{1,0:T(8,128)(2,1)S(1)} copy-done((bf16[128,1024]{1,0:T(8,128)(2,1)S(1)}, bf16[128,1024]{1,0:T(8,128)(2,1)}, u32[]{:S(2)}) %copy-start.2) | copy-done | bytes 262168
  3.6 0.0 copy-start.3
  3.6 0.9 %copy-done.3 = bf16[16,64,64]{2,1,0:T(8,128)(2,1)S(1)} copy-done((bf16[16,64,64]{2,1,0:T(8,128)(2,1)S(1)}, bf16[16,64,64]{2,1,0:T(8,128)(2,1)}, u32[]{:S(2)}) %copy-start.3) | copy-done | bytes 131096
  4.5 0.0 copy-start.4
  4.6 0.9 %copy-done.4 = bf16[64,1024]{1,0:T(8,128)(2,1)S(1)} copy-done((bf16[64,1024]{1,0:T(8,128)(2,1)S(1)}, bf16[64,1024]{1,0:T(8,128)(2,1)}, u32[]{:S(2)}) %copy-start.4) | copy-done | bytes 131096
  5.5 0.0 copy-start.5
  5.5 0.7 %copy-done.5 = bf16[128,16]{0,1:T(8,128)(2,1)S(1)} copy-done((bf16[128,16]{0,1:T(8,128)(2,1)S(1)}, bf16[128,16]{0,1:T(8,128)(2,1)}, u32[]{:S(2)}) %copy-start.5) | copy-done | bytes 4120
  6.1 0.0 copy-start.6
  6.1 0.7 %copy-done.6 = f32[1024]{0:T(1024)S(1)} copy-done((f32[1024]{0:T(1024)S(1)}, f32[1024]{0:T(1024)}, u32[]{:S(2)}) %copy-start.6) | copy-done | bytes 4120
  6.8 36.4 %shard_map.82 = bf16[64,1024]{1,0:T(8,128)(2,1)S(1)} custom-call(bf16[128,1024]{1,0:T(8,128)(2,1)S(1)} %copy-done.1, bf16[128,1024]{1,0:T(8,128)(2,1)S(1)} %copy-done.2, bf16[16,128]{1,0:T(8,128)(2,1)S(1)} %bitcast.2, bf16[64,1024]{1,0:T(8,128)(2,1)S(1)} %copy-done.4, bf16[2,16,64,64]{3,2,1,0:T(8,128)(2,1)S(1)} %copy-done, ...), custom_call_target="tpu_custom_call" | custom-call | tf_op jit(solution)/shard_map/pallas_call | solution.py:353
  43.2 0.7 %copy.10 = bf16[64,1024]{1,0:T(8,128)(2,1)} copy(bf16[64,1024]{1,0:T(8,128)(2,1)S(1)} %shard_map.82) | data formatting | bytes 262144
Async XLA Ops:
  0.0 0.7 %copy-start.7 = (f32[16]{0:T(128)S(1)}, f32[16]{0:T(128)}, u32[]{:S(2)}) copy-start(f32[16]{0:T(128)} %steps_hbm.1) | copy-start | bytes 196
  0.7 1.0 %copy-start = (bf16[2,16,64,64]{3,2,1,0:T(8,128)(2,1)S(1)}, bf16[2,16,64,64]{3,2,1,0:T(8,128)(2,1)}, u32[]{:S(2)}) copy-start(bf16[2,16,64,64]{3,2,1,0:T(8,128)(2,1)} %gate_up_hbm.1) | copy-start | bytes 786436
  1.7 0.9 %copy-start.1 = (bf16[128,1024]{1,0:T(8,128)(2,1)S(1)}, bf16[128,1024]{1,0:T(8,128)(2,1)}, u32[]{:S(2)}) copy-start(bf16[128,1024]{1,0:T(8,128)(2,1)} %keys_hbm.1) | copy-start | bytes 786436
  2.6 0.9 %copy-start.2 = (bf16[128,1024]{1,0:T(8,128)(2,1)S(1)}, bf16[128,1024]{1,0:T(8,128)(2,1)}, u32[]{:S(2)}) copy-start(bf16[128,1024]{1,0:T(8,128)(2,1)} %values_hbm.1) | copy-start | bytes 786436
  3.6 0.9 %copy-start.3 = (bf16[16,64,64]{2,1,0:T(8,128)(2,1)S(1)}, bf16[16,64,64]{2,1,0:T(8,128)(2,1)}, u32[]{:S(2)}) copy-start(bf16[16,64,64]{2,1,0:T(8,128)(2,1)} %down_t_hbm.1) | copy-start | bytes 393220
  4.5 0.9 %copy-start.4 = (bf16[64,1024]{1,0:T(8,128)(2,1)S(1)}, bf16[64,1024]{1,0:T(8,128)(2,1)}, u32[]{:S(2)}) copy-start(bf16[64,1024]{1,0:T(8,128)(2,1)} %queries_hbm.1) | copy-start | bytes 393220
  5.5 0.7 %copy-start.5 = (bf16[128,16]{0,1:T(8,128)(2,1)S(1)}, bf16[128,16]{0,1:T(8,128)(2,1)}, u32[]{:S(2)}) copy-start(bf16[128,16]{0,1:T(8,128)(2,1)} %param.10) | copy-start | bytes 12292
  6.1 0.7 %copy-start.6 = (f32[1024]{0:T(1024)S(1)}, f32[1024]{0:T(1024)}, u32[]{:S(2)}) copy-start(f32[1024]{0:T(1024)} %param.15) | copy-start | bytes 12292

commit v4 on v3

v4 whole, which is shorter than its diff:
```python
import jax
import jax.numpy as jnp
from jax import lax
from jax.experimental import pallas as pl
from jax.experimental.pallas import tpu as pltpu
from jax.sharding import PartitionSpec as P

NS_STEPS = 5
GROUP = 16
PAIRS = GROUP // 2
DH = 64
HID = 1024
LANES = 128
COLS = 256

poly_one = 3.4445
poly_two = -4.775
poly_three = 2.0315

ROWS_BY_ROWS = (((1,), (1,)), ((), ()))
COLS_BY_COLS = (((0,), (0,)), ((), ()))


def plain_dot(left, right):
    return jnp.dot(left, right, preferred_element_type=jnp.float32)


def nt_dot(left, right):
    return lax.dot_general(left, right, ROWS_BY_ROWS, preferred_element_type=jnp.float32)


def exact_dot(left, right):
    return jnp.dot(
        left, right, precision=lax.Precision.HIGHEST, preferred_element_type=jnp.float32
    )


def side_by_side(left, right):
    return jnp.concatenate([left, right], axis=1)


def clear_grads(grad):
    grad[...] = jnp.zeros_like(grad)


def unpack_weights(pair, recv_w, weight):
    even, odd = recv_w[2 * pair], recv_w[2 * pair + 1]
    cols = pl.ds(pl.multiple_of(pair * LANES, LANES), LANES)
    weight[0, :, cols] = side_by_side(even[:DH, :DH], odd[:DH, :DH])
    weight[1, :, cols] = side_by_side(even[:DH, DH:], odd[:DH, DH:])
    weight[2, : DH // 2, cols] = side_by_side(even[DH:, :DH], odd[DH:, :DH])
    weight[2, DH // 2 :, cols] = side_by_side(even[DH:, DH:], odd[DH:, DH:])


def make_terms(slot, cols, keys, errors, weight, terms):
    gate = plain_dot(keys, weight[0, :, cols])
    up = plain_dot(keys, weight[1, :, cols])
    back = plain_dot(errors, weight[2, :, cols])
    sigma = 0.5 * jnp.tanh(0.5 * gate) + 0.5
    gated = gate * sigma
    terms[slot, 0, :, cols] = (back * up * (sigma + gated * (1.0 - sigma))).astype(jnp.bfloat16)
    terms[slot, 1, :, cols] = (back * gated).astype(jnp.bfloat16)
    terms[slot, 2, :, cols] = (gated * up).astype(jnp.bfloat16)


def add_grads(slot, cols, turned, terms, grad):
    grad[0, :, cols] += plain_dot(turned[slot, :DH, :], terms[slot, 0, :, cols])
    grad[1, :, cols] += plain_dot(turned[slot, :DH, :], terms[slot, 1, :, cols])
    grad[2, :, cols] += plain_dot(turned[slot, DH:, :], terms[slot, 2, :, cols])


def grad_chunk(pair, slot, recv_t, weight, turned, terms, grad, fill=True, drain=True):
    if fill:
        block = recv_t[pl.ds(2 * pair, 2)].reshape(2 * LANES, LANES)
        turned[slot] = block.T
        keys, errors = block[:, :DH], block[:, DH:]
    for at in range(HID // COLS):
        cols = slice(at * COLS, (at + 1) * COLS)
        if fill:
            make_terms(slot, cols, keys, errors, weight, terms)
        if drain:
            add_grads(1 - slot, cols, turned, terms, grad)


def split_three(value):
    high = value.astype(jnp.bfloat16)
    rest = value - high.astype(jnp.float32)
    middle = rest.astype(jnp.bfloat16)
    low = (rest - middle.astype(jnp.float32)).astype(jnp.bfloat16)
    return high, middle, low


def orthogonalizers(pieces):
    grams, totals = [], []
    eye = (
        lax.broadcasted_iota(jnp.int32, (DH, DH), 0) == lax.broadcasted_iota(jnp.int32, (DH, DH), 1)
    ).astype(jnp.float32)
    for part in pieces:
        stacked = jnp.concatenate(part, axis=0)
        blocks = nt_dot(stacked, stacked)
        gram = sum(
            blocks[a * DH : (a + 1) * DH, b * DH : (b + 1) * DH]
            for a, b in ((1, 1), (0, 2), (2, 0), (0, 1), (1, 0), (0, 0))
        )
        square_norm = jnp.sum(gram * eye, axis=(0, 1), keepdims=True)
        factor = 1.0 / (jnp.sqrt(square_norm) + 1e-07)
        grams.append(gram * (factor * factor))
        totals.append(factor)
    for step in range(NS_STEPS):
        squares = [exact_dot(gram, gram) for gram in grams]
        blends = [
            poly_one * eye + poly_two * gram + poly_three * square
            for gram, square in zip(grams, squares)
        ]
        totals = [
            blend * total if step == 0 else exact_dot(blend, total)
            for blend, total in zip(blends, totals)
        ]
        if step < NS_STEPS - 1:
            cubes = [exact_dot(gram, square) for gram, square in zip(grams, squares)]
            halves = [
                poly_one * gram + poly_two * square + poly_three * cube
                for gram, square, cube in zip(grams, squares, cubes)
            ]
            grams = [exact_dot(half, blend) for half, blend in zip(halves, blends)]
    return totals


def renew(grad, weight, fresh, turned_down, step_size):
    pieces = [split_three(grad[part]) for part in range(3)]
    totals = orthogonalizers(pieces)
    for part in range(3):
        high, middle, _ = split_three(totals[part])
        left = jnp.concatenate([high, high, middle, middle], axis=1)
        right = jnp.concatenate([pieces[part][0], pieces[part][1]] * 2, axis=0)
        start = weight[part].astype(jnp.float32)
        moved = start - step_size * plain_dot(left, right)
        keep = jnp.sum(start * start, axis=0, keepdims=True)
        length = jnp.sum(moved * moved, axis=0, keepdims=True)
        moved = (moved * (jnp.sqrt(keep) / (jnp.sqrt(length) + 1e-06))).astype(jnp.bfloat16)
        if part < 2:
            fresh[part] = moved
        else:
            turned_down[...] = moved.T


SOURCES = 4


def apply_block(at, recv_q, fresh, turned_down, gain, send_o):
    take = pl.ds(at * SOURCES, SOURCES)
    count = SOURCES * DH // 2
    block = jnp.concatenate(
        [recv_q[take, :, :DH].reshape(count, DH), recv_q[take, :, DH:].reshape(count, DH)], axis=0
    )
    hidden = []
    for part in range(HID // COLS):
        cols = slice(part * COLS, (part + 1) * COLS)
        gate = plain_dot(block, fresh[0, :, cols])
        up = plain_dot(block, fresh[1, :, cols])
        sigma = 0.5 * jnp.tanh(0.5 * gate) + 0.5
        hidden.append((gate * sigma * up).astype(jnp.bfloat16))
    head_out = plain_dot(jnp.concatenate(hidden, axis=1), turned_down[...])
    mean_square = jnp.sum(head_out * head_out, axis=1, keepdims=True) * (1.0 / DH)
    done = head_out * lax.rsqrt(mean_square + 1e-06) * gain
    packed = side_by_side(done[:count], done[count:]).astype(jnp.bfloat16)
    send_o[take] = packed.reshape(SOURCES, DH // 2, LANES)


def pack_tokens(keys, values, rates, send_t):
    head_of = lax.broadcasted_iota(jnp.int32, (GROUP, LANES), 1) // DH
    row = lax.broadcasted_iota(jnp.int32, (GROUP, LANES), 0)
    for pair in range(PAIRS):
        cols = slice(pair * LANES, (pair + 1) * LANES)
        spread = (row == head_of + 2 * pair).astype(jnp.bfloat16)
        rate = lax.dot_general(
            rates[...], spread, COLS_BY_COLS, preferred_element_type=jnp.float32
        )
        error = (-(rate * values[:, cols].astype(jnp.float32))).astype(jnp.bfloat16)
        key = keys[:, cols]
        send_t[2 * pair] = side_by_side(key[:, :DH], error[:, :DH])
        send_t[2 * pair + 1] = side_by_side(key[:, DH:], error[:, DH:])


def pack_queries(queries, send_q):
    half = DH // 2
    for pair in range(PAIRS):
        cols = slice(pair * LANES, (pair + 1) * LANES)
        top, bottom = queries[:half, cols], queries[half:, cols]
        send_q[2 * pair] = side_by_side(top[:, :DH], bottom[:, :DH])
        send_q[2 * pair + 1] = side_by_side(top[:, DH:], bottom[:, DH:])


def pack_weights(gate_up, down_t, send_w):
    for head in range(GROUP):
        send_w[head, :DH, :] = side_by_side(gate_up[0, head], gate_up[1, head])
        down = down_t[head]
        send_w[head, DH:, :] = side_by_side(down[: DH // 2], down[DH // 2 :])


def whole_kernel(
    keys_hbm,
    values_hbm,
    rates_hbm,
    queries_hbm,
    gate_up_hbm,
    down_t_hbm,
    steps_hbm,
    gain_hbm,
    outputs,
    keys,
    values,
    rates,
    queries,
    gate_up,
    down_t,
    step_sizes,
    gain_rows,
    send_w,
    recv_w,
    send_t,
    recv_t,
    send_q,
    recv_q,
    send_o,
    recv_o,
    weight,
    turned,
    terms,
    grad,
    fresh,
    turned_down,
    out_sems,
    in_sems,
    here,
    loaded,
):
    me = lax.axis_index("view")
    my_pair, my_side = me // 2, me % 2

    def peer(step):
        return lax.rem(me + step, GROUP)

    def loop(first, count, one):
        def loop_body(at, carry):
            one(at)
            return carry

        lax.fori_loop(first, count, loop_body, 0)

    loads = [
        pltpu.make_async_copy(far, near, loaded.at[at])
        for at, (far, near) in enumerate(
            (
                (gate_up_hbm, gate_up),
                (down_t_hbm, down_t),
                (keys_hbm, keys),
                (values_hbm, values),
                (rates_hbm, rates),
                (queries_hbm, queries),
                (steps_hbm, step_sizes),
                (gain_hbm, gain_rows),
            )
        )
    ]
    for load in loads:
        load.start()

    barrier = pltpu.get_barrier_semaphore()

    def greet(step):
        pl.semaphore_signal(
            barrier,
            inc=1,
            device_id={"view": peer(step)},
            device_id_type=pl.DeviceIdType.MESH,
        )

    loop(1, GROUP, greet)

    def copy(kind, source, target_buffer):
        def build(target, origin):
            return pltpu.make_async_remote_copy(
                src_ref=source.at[target],
                dst_ref=target_buffer.at[origin],
                send_sem=out_sems.at[kind, target],
                recv_sem=in_sems.at[kind, origin],
                device_id={"view": target},
                device_id_type=pl.DeviceIdType.MESH,
            )

        return build

    w_copy = copy(0, send_w, recv_w)
    t_copy = copy(1, send_t, recv_t)
    q_copy = copy(2, send_q, recv_q)
    o_copy = copy(3, send_o, recv_o)

    for load in loads[:2]:
        load.wait()
    pack_weights(gate_up, down_t, send_w)
    pl.semaphore_wait(barrier, GROUP - 1)
    loop(1, GROUP, lambda step: w_copy(peer(step), me).start())
    for load in loads[2:5]:
        load.wait()
    pack_tokens(keys, values, rates, send_t)
    loop(1, GROUP, lambda step: t_copy(peer(step), me).start())
    for load in loads[5:]:
        load.wait()
    pack_queries(queries, send_q)
    loop(1, GROUP, lambda step: q_copy(peer(step), me).start())

    own = [
        pltpu.make_async_copy(source.at[me], target.at[me], here.at[at])
        for at, (source, target) in enumerate(
            ((send_w, recv_w), (send_t, recv_t), (send_q, recv_q))
        )
    ]
    for copied in own:
        copied.start()
    clear_grads(grad)
    for copied in own:
        copied.wait()

    loop(1, GROUP, lambda step: w_copy(peer(step), peer(step)).wait_recv())
    for pair in range(PAIRS):
        unpack_weights(pair, recv_w, weight)

    def pair_at(step):
        return lax.rem(my_pair + PAIRS - step, PAIRS)

    def take_tokens(step):
        pair = pair_at(step)
        t_copy(2 * pair, 2 * pair).wait_recv()
        t_copy(2 * pair + 1, 2 * pair + 1).wait_recv()
        return pair

    other = my_pair * 2 + 1 - my_side
    t_copy(other, other).wait_recv()
    grad_chunk(my_pair, 0, recv_t, weight, turned, terms, grad, drain=False)

    def two_chunks(at):
        for side in range(2):
            pair = take_tokens(2 * at + 1 + side)
            grad_chunk(pair, 1 - side, recv_t, weight, turned, terms, grad)

    loop(0, PAIRS // 2 - 1, two_chunks)
    grad_chunk(take_tokens(PAIRS - 1), 1, recv_t, weight, turned, terms, grad)
    grad_chunk(0, 0, recv_t, weight, turned, terms, grad, fill=False)

    renew(grad, weight, fresh, turned_down, step_sizes[me])
    gain = gain_rows[pl.ds(my_pair, 1), :]
    gain = jnp.where(my_side == 0, gain[:, :DH], gain[:, DH:])
    loop(1, GROUP, lambda step: q_copy(peer(step), peer(step)).wait_recv())

    for at in range(GROUP // SOURCES):
        apply_block(at, recv_q, fresh, turned_down, gain, send_o)
        for target in range(at * SOURCES, (at + 1) * SOURCES):

            @pl.when(target != me)
            def _():
                o_copy(target, me).start()

    own_o = pltpu.make_async_copy(send_o.at[me], recv_o.at[me], here.at[3])
    own_o.start()
    own_o.wait()
    loop(1, GROUP, lambda step: o_copy(peer(step), peer(step)).wait_recv())
    half = DH // 2
    for pair in range(PAIRS):
        even, odd = recv_o[2 * pair], recv_o[2 * pair + 1]
        cols = slice(pair * LANES, (pair + 1) * LANES)
        outputs[:half, cols] = side_by_side(even[:, :DH], odd[:, :DH])
        outputs[half:, cols] = side_by_side(even[:, DH:], odd[:, DH:])

    def finish_sends(step):
        for build in (w_copy, t_copy, q_copy, o_copy):
            build(peer(step), me).wait_send()

    loop(1, GROUP, finish_sends)


def shards(keys, values, rates, queries, gate_up, down_t, step_sizes, gain):
    bf16, f32 = jnp.bfloat16, jnp.float32

    def boxes(rows):
        return [pltpu.VMEM((GROUP, rows, LANES), bf16)] * 2

    return pl.pallas_call(
        whole_kernel,
        out_shape=jax.ShapeDtypeStruct(queries.shape, bf16),
        in_specs=[pl.BlockSpec(memory_space=pltpu.HBM)] * 8,
        out_specs=pl.BlockSpec(memory_space=pltpu.VMEM),
        scratch_shapes=[
            pltpu.VMEM(keys.shape, bf16),
            pltpu.VMEM(values.shape, bf16),
            pltpu.VMEM(rates.shape[::-1], bf16),
            pltpu.VMEM(queries.shape, bf16),
            pltpu.VMEM(gate_up.shape, bf16),
            pltpu.VMEM(down_t.shape, bf16),
            pltpu.SMEM(step_sizes.shape, f32),
            pltpu.VMEM((PAIRS, LANES), f32),
        ]
        + boxes(DH + DH // 2)
        + boxes(LANES)
        + boxes(DH // 2)
        + boxes(DH // 2)
        + [
            pltpu.VMEM((3, DH, HID), bf16),
            pltpu.VMEM((2, 2 * DH, 2 * LANES), bf16),
            pltpu.VMEM((2, 3, 2 * LANES, HID), bf16),
            pltpu.VMEM((3, DH, HID), f32),
            pltpu.VMEM((2, DH, HID), bf16),
            pltpu.VMEM((HID, DH), bf16),
            pltpu.SemaphoreType.DMA((4, GROUP)),
            pltpu.SemaphoreType.DMA((4, GROUP)),
            pltpu.SemaphoreType.DMA((4,)),
            pltpu.SemaphoreType.DMA((8,)),
        ],
        compiler_params=pltpu.CompilerParams(
            collective_id=0, has_side_effects=True, vmem_limit_bytes=60 << 20
        ),
    )(
        keys,
        values,
        rates.T,
        queries,
        gate_up,
        down_t,
        step_sizes,
        gain.reshape(PAIRS, LANES),
    )


def solution(mesh):
    return jax.shard_map(
        shards,
        mesh=mesh,
        in_specs=(
            P(("scene", "view"), None),
            P(("scene", "view"), None),
            P(("scene", "view"), None),
            P(("scene", "view"), None),
            P(None, None, None, "view"),
            P(None, None, "view"),
            P(),
            P(),
        ),
        out_specs=P(("scene", "view"), None),
        check_vma=False,
    )
```

time: 44.2 us -> 34.3 us (0.78)
  local copies, waits for them, and re-layouts: 7.48 us -> 1.57 us
  Pallas kernels: 36.4 us -> 32.6 us
    unnamed x17 -> x1, local copies, waits for them, and re-layouts: 7.48 us -> 1.57 us
    pallas_call x1, Pallas kernels: 36.4 us -> 32.6 us  [shards(): pl.pallas_call(whole_kernel, out_shape=jax.ShapeDtypeStruct(queries.shape...]
where the time goes in v4:
time: 34.3 us; the launch traced here: 34.2 us
  Pallas kernels  32.6 us (95%)
  local copies, waits for them, and re-layouts  1.57 us (5%)
    pallas_call x1, Pallas kernels, shards(): pl.pallas_call(whole_kernel, out_shape=jax.ShapeDtypeStruct(queries.shape...  32.6 us
    unnamed x1, local copies, waits for them, and re-layouts  1.57 us

profile of v4, /device:TPU:1, one launch (start us, length us, event | category | flops | bytes accessed | tf_op | source)
XLA Modules:
  0.0 34.2 jit_solution(17275862582004173151)
XLA Ops:
  0.0 32.6 %shard_map.82 = bf16[64,1024]{1,0:T(8,128)(2,1)} custom-call(bf16[128,1024]{1,0:T(8,128)(2,1)} %keys_hbm.1, bf16[128,1024]{1,0:T(8,128)(2,1)} %values_hbm.1, bf16[16,128]{1,0:T(8,128)(2,1)} %bitcast.2, bf16[64,1024]{1,0:T(8,128)(2,1)} %queries_hbm.1, bf16[2,16,64,64]{3,2,1,0:T(8,128)(2,1)} %gate_up_hbm.1, bf16[16,64,64]{2,1,0:T(8,128)(2,1)} %down_t_hbm.1, ...), custom_call_target="tpu_custom_call" | custom-call | tf_op jit(solution)/shard_map/pallas_call | solution.py:388
  32.6 1.6 %copy.10 = bf16[64,1024]{1,0:T(8,128)(2,1)} copy(bf16[64,1024]{1,0:T(8,128)(2,1)} %shard_map.82) | data formatting | bytes 262144

commit v5 on v4

--- a/solution.py
+++ b/solution.py
@@ -27,12 +27,6 @@
 
 def nt_dot(left, right):
     return lax.dot_general(left, right, ROWS_BY_ROWS, preferred_element_type=jnp.float32)
-
-
-def exact_dot(left, right):
-    return jnp.dot(
-        left, right, precision=lax.Precision.HIGHEST, preferred_element_type=jnp.float32
-    )
 
 
 def side_by_side(left, right):
@@ -90,39 +84,66 @@
     return high, middle, low
 
 
+def twin(value):
+    return side_by_side(value, value)
+
+
+def first_half(shape):
+    return lax.broadcasted_iota(jnp.int32, shape, 1) < DH
+
+
+def exact_twins(left, right):
+    high, middle, low = left
+    near = first_half(high.shape)
+    wide = jnp.concatenate(
+        [high, jnp.where(near, middle, high), jnp.where(near, middle, low)], axis=1
+    )
+    high, middle, low = right
+    tall = jnp.concatenate([high, middle, high, low, middle, high], axis=0)
+    return plain_dot(wide, tall)
+
+
+def start_gram(part):
+    high, middle, low = part
+    stacked = jnp.concatenate([high, middle, low], axis=0)
+    blocks = nt_dot(stacked, stacked)
+    main = blocks[:DH, :LANES] + blocks[DH : 2 * DH, :LANES]
+    side = blocks[2 * DH :, :DH] + blocks[:DH, 2 * DH :]
+    return twin(main[:, :DH] + (main[:, DH:] + side))
+
+
 def orthogonalizers(pieces):
+    shape = (DH, 2 * DH)
+    row = lax.broadcasted_iota(jnp.int32, shape, 0)
+    eye = (row == lax.broadcasted_iota(jnp.int32, shape, 1) % DH).astype(jnp.float32)
     grams, totals = [], []
-    eye = (
-        lax.broadcasted_iota(jnp.int32, (DH, DH), 0) == lax.broadcasted_iota(jnp.int32, (DH, DH), 1)
-    ).astype(jnp.float32)
     for part in pieces:
-        stacked = jnp.concatenate(part, axis=0)
-        blocks = nt_dot(stacked, stacked)
-        gram = sum(
-            blocks[a * DH : (a + 1) * DH, b * DH : (b + 1) * DH]
-            for a, b in ((1, 1), (0, 2), (2, 0), (0, 1), (1, 0), (0, 0))
-        )
-        square_norm = jnp.sum(gram * eye, axis=(0, 1), keepdims=True)
+        gram = start_gram(part)
+        square_norm = 0.5 * jnp.sum(gram * eye, axis=(0, 1), keepdims=True)
         factor = 1.0 / (jnp.sqrt(square_norm) + 1e-07)
         grams.append(gram * (factor * factor))
         totals.append(factor)
     for step in range(NS_STEPS):
-        squares = [exact_dot(gram, gram) for gram in grams]
+        cut = [split_three(gram) for gram in grams]
+        squares = [exact_twins(one, one) for one in cut]
         blends = [
             poly_one * eye + poly_two * gram + poly_three * square
             for gram, square in zip(grams, squares)
         ]
-        totals = [
-            blend * total if step == 0 else exact_dot(blend, total)
-            for blend, total in zip(blends, totals)
-        ]
+        cut_blends = [split_three(blend) for blend in blends]
         if step < NS_STEPS - 1:
-            cubes = [exact_dot(gram, square) for gram, square in zip(grams, squares)]
+            cubes = [exact_twins(one, split_three(square)) for one, square in zip(cut, squares)]
             halves = [
                 poly_one * gram + poly_two * square + poly_three * cube
                 for gram, square, cube in zip(grams, squares, cubes)
             ]
-            grams = [exact_dot(half, blend) for half, blend in zip(halves, blends)]
+            grams = [
+                exact_twins(split_three(half), blend) for half, blend in zip(halves, cut_blends)
+            ]
+        totals = [
+            blend * total if step == 0 else exact_twins(cut_blend, split_three(total))
+            for blend, cut_blend, total in zip(blends, cut_blends, totals)
+        ]
     return totals
 
 
@@ -131,10 +152,9 @@
     totals = orthogonalizers(pieces)
     for part in range(3):
         high, middle, _ = split_three(totals[part])
-        left = jnp.concatenate([high, high, middle, middle], axis=1)
         right = jnp.concatenate([pieces[part][0], pieces[part][1]] * 2, axis=0)
         start = weight[part].astype(jnp.float32)
-        moved = start - step_size * plain_dot(left, right)
+        moved = start - step_size * plain_dot(side_by_side(high, middle), right)
         keep = jnp.sum(start * start, axis=0, keepdims=True)
         length = jnp.sum(moved * moved, axis=0, keepdims=True)
         moved = (moved * (jnp.sqrt(keep) / (jnp.sqrt(length) + 1e-06))).astype(jnp.bfloat16)
@@ -237,9 +257,14 @@
 ):
     me = lax.axis_index("view")
     my_pair, my_side = me // 2, me % 2
+    my_row, my_depth = me // 4, my_pair % 2
+    partner = 2 * my_pair + 1 - my_side
 
     def peer(step):
         return lax.rem(me + step, GROUP)
+
+    def chip(rows, depth):
+        return ((my_row + rows) % 4) * 2 + (my_depth + depth) % 2
 
     def loop(first, count, one):
         def loop_body(at, carry):
@@ -268,15 +293,28 @@
 
     barrier = pltpu.get_barrier_semaphore()
 
-    def greet(step):
+    def greet(target):
         pl.semaphore_signal(
-            barrier,
-            inc=1,
-            device_id={"view": peer(step)},
-            device_id_type=pl.DeviceIdType.MESH,
+            barrier, inc=1, device_id={"view": target}, device_id_type=pl.DeviceIdType.MESH
         )
 
-    loop(1, GROUP, greet)
+    for rows in (2, 1, 3, 0):
+        for depth in (1, 0):
+            if rows or depth:
+                greet(2 * chip(rows, depth))
+                greet(2 * chip(rows, depth) + 1)
+    greet(partner)
+
+    def to_all(build):
+        build(partner, me).start()
+
+        def send(step):
+            there = PAIRS - step
+            pair = chip(4 - there // 2, there % 2)
+            build(2 * pair, me).start()
+            build(2 * pair + 1, me).start()
+
+        loop(1, PAIRS, send)
 
     def copy(kind, source, target_buffer):
         def build(target, origin):
@@ -300,15 +338,15 @@
         load.wait()
     pack_weights(gate_up, down_t, send_w)
     pl.semaphore_wait(barrier, GROUP - 1)
-    loop(1, GROUP, lambda step: w_copy(peer(step), me).start())
+    to_all(w_copy)
     for load in loads[2:5]:
         load.wait()
     pack_tokens(keys, values, rates, send_t)
-    loop(1, GROUP, lambda step: t_copy(peer(step), me).start())
+    to_all(t_copy)
     for load in loads[5:]:
         load.wait()
     pack_queries(queries, send_q)
-    loop(1, GROUP, lambda step: q_copy(peer(step), me).start())
+    to_all(q_copy)
 
     own = [
         pltpu.make_async_copy(source.at[me], target.at[me], here.at[at])
@@ -326,17 +364,14 @@
     for pair in range(PAIRS):
         unpack_weights(pair, recv_w, weight)
 
-    def pair_at(step):
-        return lax.rem(my_pair + PAIRS - step, PAIRS)
-
     def take_tokens(step):
-        pair = pair_at(step)
+        there = PAIRS - step
+        pair = chip(there // 2, there % 2)
         t_copy(2 * pair, 2 * pair).wait_recv()
         t_copy(2 * pair + 1, 2 * pair + 1).wait_recv()
         return pair
 
-    other = my_pair * 2 + 1 - my_side
-    t_copy(other, other).wait_recv()
+    t_copy(partner, partner).wait_recv()
     grad_chunk(my_pair, 0, recv_t, weight, turned, terms, grad, drain=False)
 
     def two_chunks(at):
@@ -353,16 +388,23 @@
     gain = jnp.where(my_side == 0, gain[:, :DH], gain[:, DH:])
     loop(1, GROUP, lambda step: q_copy(peer(step), peer(step)).wait_recv())
 
-    for at in range(GROUP // SOURCES):
-        apply_block(at, recv_q, fresh, turned_down, gain, send_o)
-        for target in range(at * SOURCES, (at + 1) * SOURCES):
-
-            @pl.when(target != me)
-            def _():
-                o_copy(target, me).start()
-
+    for rows in (2, 1, 3, 0):
+        block = (my_row + rows) % 4
+        apply_block(block, recv_q, fresh, turned_down, gain, send_o)
+        for depth in (1, 0):
+            pair = chip(rows, depth)
+            if rows or depth:
+                o_copy(2 * pair, me).start()
+                o_copy(2 * pair + 1, me).start()
+    o_copy(partner, me).start()
     own_o = pltpu.make_async_copy(send_o.at[me], recv_o.at[me], here.at[3])
     own_o.start()
+
+    def finish_sends(step):
+        for build in (w_copy, t_copy, q_copy, o_copy):
+            build(peer(step), me).wait_send()
+
+    loop(1, GROUP, finish_sends)
     own_o.wait()
     loop(1, GROUP, lambda step: o_copy(peer(step), peer(step)).wait_recv())
     half = DH // 2
@@ -372,12 +414,6 @@
         outputs[:half, cols] = side_by_side(even[:, :DH], odd[:, :DH])
         outputs[half:, cols] = side_by_side(even[:, DH:], odd[:, DH:])
 
-    def finish_sends(step):
-        for build in (w_copy, t_copy, q_copy, o_copy):
-            build(peer(step), me).wait_send()
-
-    loop(1, GROUP, finish_sends)
-
 
 def shards(keys, values, rates, queries, gate_up, down_t, step_sizes, gain):
     bf16, f32 = jnp.bfloat16, jnp.float32
@@ -387,7 +423,7 @@
 
     return pl.pallas_call(
         whole_kernel,
-        out_shape=jax.ShapeDtypeStruct(queries.shape, bf16),
+        out_shape=pltpu.VMEM(queries.shape, bf16),
         in_specs=[pl.BlockSpec(memory_space=pltpu.HBM)] * 8,
         out_specs=pl.BlockSpec(memory_space=pltpu.VMEM),
         scratch_shapes=[

time: 34.3 us -> 32.6 us (0.950)
  local copies, waits for them, and re-layouts: 1.57 us -> 0.66 us
  Pallas kernels: 32.6 us -> 31.9 us
    unnamed x1, local copies, waits for them, and re-layouts: 1.57 us -> 0.66 us
    pallas_call x1, Pallas kernels: 32.6 us -> 31.9 us  [shards(): pl.pallas_call(whole_kernel, out_shape=pltpu.VMEM(queries.shape, bf16), i...]
where the time goes in v5:
time: 32.6 us; the launch traced here: 32.5 us
  Pallas kernels  31.9 us (98%)
  local copies, waits for them, and re-layouts  0.66 us (2%)
    pallas_call x1, Pallas kernels, shards(): pl.pallas_call(whole_kernel, out_shape=pltpu.VMEM(queries.shape, bf16), i...  31.9 us
    unnamed x1, local copies, waits for them, and re-layouts  0.66 us

profile of v5, /device:TPU:1, one launch (start us, length us, event | category | flops | bytes accessed | tf_op | source)
XLA Modules:
  0.0 32.5 jit_solution(6952268428087583770)
XLA Ops:
  0.0 31.9 %shard_map.82 = bf16[64,1024]{1,0:T(8,128)(2,1)S(1)} custom-call(bf16[128,1024]{1,0:T(8,128)(2,1)} %keys_hbm.1, bf16[128,1024]{1,0:T(8,128)(2,1)} %values_hbm.1, bf16[16,128]{1,0:T(8,128)(2,1)} %bitcast.2, bf16[64,1024]{1,0:T(8,128)(2,1)} %queries_hbm.1, bf16[2,16,64,64]{3,2,1,0:T(8,128)(2,1)} %gate_up_hbm.1, bf16[16,64,64]{2,1,0:T(8,128)(2,1)} %down_t_hbm.1, ...), custom_call_target="tpu_custom_call" | custom-call | tf_op jit(solution)/shard_map/pallas_call | solution.py:424
  31.9 0.7 %copy.10 = bf16[64,1024]{1,0:T(8,128)(2,1)} copy(bf16[64,1024]{1,0:T(8,128)(2,1)S(1)} %shard_map.82) | data formatting | bytes 262144

commit v6 on v5

--- a/solution.py
+++ b/solution.py
@@ -305,16 +305,15 @@
                 greet(2 * chip(rows, depth) + 1)
     greet(partner)
 
-    def to_all(build):
+    T_ORDER = [(3, 0), (1, 1), (3, 1), (1, 0), (2, 0), (0, 1), (2, 1)]
+    W_ORDER = [(3, 0), (1, 1), (3, 1), (1, 0), (2, 0), (0, 1), (2, 1)]
+
+    def to_all(build, order=W_ORDER):
         build(partner, me).start()
-
-        def send(step):
-            there = PAIRS - step
-            pair = chip(4 - there // 2, there % 2)
+        for rows, depth in order:
+            pair = chip(-rows % 4, depth)
             build(2 * pair, me).start()
             build(2 * pair + 1, me).start()
-
-        loop(1, PAIRS, send)
 
     def copy(kind, source, target_buffer):
         def build(target, origin):
@@ -337,16 +336,15 @@
     for load in loads[:2]:
         load.wait()
     pack_weights(gate_up, down_t, send_w)
-    pl.semaphore_wait(barrier, GROUP - 1)
-    to_all(w_copy)
     for load in loads[2:5]:
         load.wait()
     pack_tokens(keys, values, rates, send_t)
-    to_all(t_copy)
     for load in loads[5:]:
         load.wait()
     pack_queries(queries, send_q)
-    to_all(q_copy)
+    pl.semaphore_wait(barrier, GROUP - 1)
+    to_all(w_copy)
+    to_all(t_copy, T_ORDER)
 
     own = [
         pltpu.make_async_copy(source.at[me], target.at[me], here.at[at])
@@ -365,29 +363,24 @@
         unpack_weights(pair, recv_w, weight)
 
     def take_tokens(step):
-        there = PAIRS - step
-        pair = chip(there // 2, there % 2)
+        pair = chip(*T_ORDER[step])
         t_copy(2 * pair, 2 * pair).wait_recv()
         t_copy(2 * pair + 1, 2 * pair + 1).wait_recv()
         return pair
 
     t_copy(partner, partner).wait_recv()
     grad_chunk(my_pair, 0, recv_t, weight, turned, terms, grad, drain=False)
-
-    def two_chunks(at):
-        for side in range(2):
-            pair = take_tokens(2 * at + 1 + side)
-            grad_chunk(pair, 1 - side, recv_t, weight, turned, terms, grad)
-
-    loop(0, PAIRS // 2 - 1, two_chunks)
-    grad_chunk(take_tokens(PAIRS - 1), 1, recv_t, weight, turned, terms, grad)
+    for step in range(7):
+        grad_chunk(take_tokens(step), 1 - step % 2, recv_t, weight, turned, terms, grad)
+        if step == 1:
+            to_all(q_copy)
     grad_chunk(0, 0, recv_t, weight, turned, terms, grad, fill=False)
 
     renew(grad, weight, fresh, turned_down, step_sizes[me])
     gain = gain_rows[pl.ds(my_pair, 1), :]
     gain = jnp.where(my_side == 0, gain[:, :DH], gain[:, DH:])
+
     loop(1, GROUP, lambda step: q_copy(peer(step), peer(step)).wait_recv())
-
     for rows in (2, 1, 3, 0):
         block = (my_row + rows) % 4
         apply_block(block, recv_q, fresh, turned_down, gain, send_o)
@@ -406,13 +399,19 @@
 
     loop(1, GROUP, finish_sends)
     own_o.wait()
-    loop(1, GROUP, lambda step: o_copy(peer(step), peer(step)).wait_recv())
     half = DH // 2
-    for pair in range(PAIRS):
-        even, odd = recv_o[2 * pair], recv_o[2 * pair + 1]
-        cols = slice(pair * LANES, (pair + 1) * LANES)
-        outputs[:half, cols] = side_by_side(even[:, :DH], odd[:, :DH])
-        outputs[half:, cols] = side_by_side(even[:, DH:], odd[:, DH:])
+    for rows in (2, 3, 1, 0):
+        for depth in range(2):
+            pair = chip(rows, depth)
+            for side in range(2):
+                if rows or depth:
+                    o_copy(2 * pair + side, 2 * pair + side).wait_recv()
+                elif side:
+                    o_copy(partner, partner).wait_recv()
+            even, odd = recv_o[2 * pair], recv_o[2 * pair + 1]
+            cols = pl.ds(pl.multiple_of(pair * LANES, LANES), LANES)
+            outputs[:half, cols] = side_by_side(even[:, :DH], odd[:, :DH])
+            outputs[half:, cols] = side_by_side(even[:, DH:], odd[:, DH:])
 
 
 def shards(keys, values, rates, queries, gate_up, down_t, step_sizes, gain):

time: 32.6 us -> 31.1 us (0.954)
  Pallas kernels: 31.9 us -> 30.3 us
    pallas_call x1, Pallas kernels: 31.9 us -> 30.3 us  [shards(): pl.pallas_call(whole_kernel, out_shape=pltpu.VMEM(queries.shape, bf16), i...]
where the time goes in v6:
time: 31.1 us; the launch traced here: 31 us
  Pallas kernels  30.3 us (97%)
  local copies, waits for them, and re-layouts  0.66 us (2%)
    pallas_call x1, Pallas kernels, shards(): pl.pallas_call(whole_kernel, out_shape=pltpu.VMEM(queries.shape, bf16), i...  30.3 us
    unnamed x1, local copies, waits for them, and re-layouts  0.66 us

profile of v6, /device:TPU:1, one launch (start us, length us, event | category | flops | bytes accessed | tf_op | source)
XLA Modules:
  0.0 31.0 jit_solution(12808231358974018369)
XLA Ops:
  0.0 30.3 %shard_map.82 = bf16[64,1024]{1,0:T(8,128)(2,1)S(1)} custom-call(bf16[128,1024]{1,0:T(8,128)(2,1)} %keys_hbm.1, bf16[128,1024]{1,0:T(8,128)(2,1)} %values_hbm.1, bf16[16,128]{1,0:T(8,128)(2,1)} %bitcast.2, bf16[64,1024]{1,0:T(8,128)(2,1)} %queries_hbm.1, bf16[2,16,64,64]{3,2,1,0:T(8,128)(2,1)} %gate_up_hbm.1, bf16[16,64,64]{2,1,0:T(8,128)(2,1)} %down_t_hbm.1, ...), custom_call_target="tpu_custom_call" | custom-call | tf_op jit(solution)/shard_map/pallas_call | solution.py:423
  30.4 0.7 %copy.10 = bf16[64,1024]{1,0:T(8,128)(2,1)} copy(bf16[64,1024]{1,0:T(8,128)(2,1)S(1)} %shard_map.82) | data formatting | bytes 262144

commit v7 on v6

--- a/solution.py
+++ b/solution.py
@@ -305,15 +305,18 @@
                 greet(2 * chip(rows, depth) + 1)
     greet(partner)
 
-    T_ORDER = [(3, 0), (1, 1), (3, 1), (1, 0), (2, 0), (0, 1), (2, 1)]
+    T_ORDER = [(3, 0), (1, 0), (0, 1), (3, 1), (1, 1), (2, 0), (2, 1)]
+    W_SENT = [(3, 0, 0), (1, 1, 0), (3, 0, 1), (1, 1, 1), (3, 1, 0), (1, 0, 0), (3, 1, 1), (1, 0, 1), (2, 0, 0), (0, 1, 0), (2, 0, 1), (0, 1, 1), (2, 1, 0), (2, 1, 1)]
+    T_SENT = [(3, 0, 0), (1, 0, 0), (0, 1, 0), (3, 0, 1), (1, 0, 1), (0, 1, 1), (3, 1, 0), (1, 1, 0), (3, 1, 1), (1, 1, 1), (2, 0, 0), (2, 1, 0), (2, 0, 1), (2, 1, 1)]
     W_ORDER = [(3, 0), (1, 1), (3, 1), (1, 0), (2, 0), (0, 1), (2, 1)]
 
-    def to_all(build, order=W_ORDER):
+    def send_to(build, places):
+        for rows, depth, side in places:
+            build(2 * chip(-rows % 4, depth) + side, me).start()
+
+    def to_all(build, order=None):
         build(partner, me).start()
-        for rows, depth in order:
-            pair = chip(-rows % 4, depth)
-            build(2 * pair, me).start()
-            build(2 * pair + 1, me).start()
+        send_to(build, W_SENT if order is None else T_SENT)
 
     def copy(kind, source, target_buffer):
         def build(target, origin):

time: 31.1 us -> 30.9 us (level)
  no operation moved by 1% of the time
where the time goes in v7:
time: 30.9 us; the launch traced here: 30.8 us
  Pallas kernels  30.1 us (97%)
  local copies, waits for them, and re-layouts  0.66 us (2%)
    pallas_call x1, Pallas kernels, shards(): pl.pallas_call(whole_kernel, out_shape=pltpu.VMEM(queries.shape, bf16), i...  30.1 us
    unnamed x1, local copies, waits for them, and re-layouts  0.66 us

profile of v7, /device:TPU:1, one launch (start us, length us, event | category | flops | bytes accessed | tf_op | source)
XLA Modules:
  0.0 30.8 jit_solution(11921240375657562191)
XLA Ops:
  0.0 30.1 %shard_map.82 = bf16[64,1024]{1,0:T(8,128)(2,1)S(1)} custom-call(bf16[128,1024]{1,0:T(8,128)(2,1)} %keys_hbm.1, bf16[128,1024]{1,0:T(8,128)(2,1)} %values_hbm.1, bf16[16,128]{1,0:T(8,128)(2,1)} %bitcast.2, bf16[64,1024]{1,0:T(8,128)(2,1)} %queries_hbm.1, bf16[2,16,64,64]{3,2,1,0:T(8,128)(2,1)} %gate_up_hbm.1, bf16[16,64,64]{2,1,0:T(8,128)(2,1)} %down_t_hbm.1, ...), custom_call_target="tpu_custom_call" | custom-call | tf_op jit(solution)/shard_map/pallas_call | solution.py:426
  30.1 0.7 %copy.10 = bf16[64,1024]{1,0:T(8,128)(2,1)} copy(bf16[64,1024]{1,0:T(8,128)(2,1)S(1)} %shard_map.82) | data formatting | bytes 262144

commit v8 on v7

--- a/solution.py
+++ b/solution.py
@@ -63,7 +63,7 @@
     grad[2, :, cols] += plain_dot(turned[slot, DH:, :], terms[slot, 2, :, cols])
 
 
-def grad_chunk(pair, slot, recv_t, weight, turned, terms, grad, fill=True, drain=True):
+def grad_chunk(pair, slot, recv_t, weight, turned, terms, grad, fill=True, drain=True, last=False):
     if fill:
         block = recv_t[pl.ds(2 * pair, 2)].reshape(2 * LANES, LANES)
         turned[slot] = block.T
@@ -74,6 +74,10 @@
             make_terms(slot, cols, keys, errors, weight, terms)
         if drain:
             add_grads(1 - slot, cols, turned, terms, grad)
+        if last and at:
+            add_grads(slot, slice((at - 1) * COLS, at * COLS), turned, terms, grad)
+    if last:
+        add_grads(slot, slice(HID - COLS, HID), turned, terms, grad)
 
 
 def split_three(value):
@@ -361,8 +365,12 @@
     for copied in own:
         copied.wait()
 
-    loop(1, GROUP, lambda step: w_copy(peer(step), peer(step)).wait_recv())
-    for pair in range(PAIRS):
+    w_copy(partner, partner).wait_recv()
+    unpack_weights(my_pair, recv_w, weight)
+    for rows, depth in W_ORDER:
+        pair = chip(rows, depth)
+        w_copy(2 * pair, 2 * pair).wait_recv()
+        w_copy(2 * pair + 1, 2 * pair + 1).wait_recv()
         unpack_weights(pair, recv_w, weight)
 
     def take_tokens(step):
@@ -374,10 +382,11 @@
     t_copy(partner, partner).wait_recv()
     grad_chunk(my_pair, 0, recv_t, weight, turned, terms, grad, drain=False)
     for step in range(7):
-        grad_chunk(take_tokens(step), 1 - step % 2, recv_t, weight, turned, terms, grad)
+        grad_chunk(
+            take_tokens(step), 1 - step % 2, recv_t, weight, turned, terms, grad, last=step == 6
+        )
         if step == 1:
             to_all(q_copy)
-    grad_chunk(0, 0, recv_t, weight, turned, terms, grad, fill=False)
 
     renew(grad, weight, fresh, turned_down, step_sizes[me])
     gain = gain_rows[pl.ds(my_pair, 1), :]

time: 30.9 us -> 30.9 us (level)
  no operation moved by 1% of the time
where the time goes in v8:
time: 30.9 us; the launch traced here: 30.8 us
  Pallas kernels  30.1 us (97%)
  local copies, waits for them, and re-layouts  0.66 us (2%)
    pallas_call x1, Pallas kernels, shards(): pl.pallas_call(whole_kernel, out_shape=pltpu.VMEM(queries.shape, bf16), i...  30.1 us
    unnamed x1, local copies, waits for them, and re-layouts  0.66 us

profile of v8, /device:TPU:1, one launch (start us, length us, event | category | flops | bytes accessed | tf_op | source)
XLA Modules:
  0.0 30.8 jit_solution(12069596997752116872)
XLA Ops:
  0.0 30.1 %shard_map.82 = bf16[64,1024]{1,0:T(8,128)(2,1)S(1)} custom-call(bf16[128,1024]{1,0:T(8,128)(2,1)} %keys_hbm.1, bf16[128,1024]{1,0:T(8,128)(2,1)} %values_hbm.1, bf16[16,128]{1,0:T(8,128)(2,1)} %bitcast.2, bf16[64,1024]{1,0:T(8,128)(2,1)} %queries_hbm.1, bf16[2,16,64,64]{3,2,1,0:T(8,128)(2,1)} %gate_up_hbm.1, bf16[16,64,64]{2,1,0:T(8,128)(2,1)} %down_t_hbm.1, ...), custom_call_target="tpu_custom_call" | custom-call | tf_op jit(solution)/shard_map/pallas_call | solution.py:435
  30.2 0.7 %copy.10 = bf16[64,1024]{1,0:T(8,128)(2,1)} copy(bf16[64,1024]{1,0:T(8,128)(2,1)S(1)} %shard_map.82) | data formatting | bytes 262144
